TPU v7x, 256 devices: a whole 4x4x8 slice. The times are simulated.
256 devices in a mesh: ctx: 8 (over x_hi, y), exp: 32 (over z, x_lo, core).
Axes of the slice: x: 4 (x_hi: 2, x_lo: 2; x = x_hi * 2 + x_lo), y: 4, z: 8, core: 2. Of those that a mesh axis runs over, the one named last changes fastest.
Arguments:
- stream_in: bfloat16 [2048, 4096], P(('ctx', 'exp')), may hold values from -4 to 4
- queries: bfloat16 [2048, 4096], P('ctx', 'exp')
- keys: bfloat16 [2048, 4096], P('ctx', 'exp')
- values: bfloat16 [2048, 4096], P('ctx', 'exp'), may hold values from -6 to 6
- w_out: bfloat16 [4096, 4096], P('exp'), may hold values from -0.5 to 0.5
- norm_gain: float32 [4096], replicated, may hold values from 0.25 to 1.75
- expert_ids: int32 [2048, 6], P(('ctx', 'exp')), may hold values from 0 to 63, all different within a row; in each aligned block of 8 rows (0 to 7, 8 to 15, ...) at most 2 rows name the same one
- gates: float32 [2048, 6], P(('ctx', 'exp')), may hold values from 0.1 to 1
- w_gate: bfloat16 [8, 32, 352, 4096], P('ctx', 'exp'), may hold values from -0.09375 to 0.09375
- w_up: bfloat16 [8, 32, 352, 4096], P('ctx', 'exp'), may hold values from -0.09375 to 0.09375
- w_down: bfloat16 [8, 32, 352, 4096], P('ctx', 'exp'), may hold values from -0.15625 to 0.15625
Outputs:
- layer_out: bfloat16 [2048, 4096], P(('ctx', 'exp'))
Inputs may be any that keep to these rules, and one draw needn't show every extreme that they name: `expert_ids`: among the 8 tokens of one device (aligned blocks of rows), no expert is named by more than 2 of them; in every draw some expert is named by exactly 2 in some block.
All inputs are finite; a program needn't handle non-finite values.
Results may differ from a plain program's by a relative error of at most 0.03.
Values may be sent and summed in bfloat16 or wider, within the bound.
No kernel may reach another device: no remote copies, remote signals or barrier semaphores. Data moves between devices by JAX's collectives and lax.ppermute only.
A program may use at most 128 MiB of HBM per device.

v0:
```python
import jax
import jax.numpy as jnp
from jax import lax
from jax.sharding import PartitionSpec as P

PIECES = 4


masked_score = -1e30


def partial_attention(query_block, query_start, key_block, value_block, key_start):
    scale = query_block.shape[1] ** (-0.5)
    scores = (
        lax.dot_general(
            query_block, key_block, (((1,), (1,)), ((), ())), preferred_element_type=jnp.float32
        )
        * scale
    )
    query_pos = query_start + jnp.arange(query_block.shape[0], dtype=jnp.int32)
    key_pos = key_start + jnp.arange(key_block.shape[0], dtype=jnp.int32)
    visible = key_pos[None, :] <= query_pos[:, None]
    scores = jnp.where(visible, scores, masked_score)
    valid = jnp.any(visible, axis=1)
    top = jnp.where(valid, jnp.max(scores, axis=1), 0.0)
    weights = jnp.where(visible, jnp.exp(scores - top[:, None]), 0.0)
    total = jnp.where(valid, jnp.sum(weights, axis=1), 1.0)
    probs = (weights / total[:, None]).astype(jnp.bfloat16)
    partial_out = jnp.dot(probs, value_block, preferred_element_type=jnp.float32)
    log_total = jnp.where(valid, top + jnp.log(total), masked_score)
    return (partial_out, log_total)


def merge_partials(outs, log_totals):
    top = jnp.max(log_totals, axis=0)
    scaled = jnp.exp(log_totals - top[None, :])
    share = scaled / jnp.sum(scaled, axis=0)[None, :]
    return jnp.sum(outs * share[:, :, None], axis=0).astype(jnp.bfloat16)


def on_device(
    stream_in, queries, keys, values, w_out, norm_gain, expert_ids, gates, w_gate, w_up, w_down
):
    shard = queries.shape[0]
    head_size = queries.shape[1]
    ctx_count = lax.axis_size("ctx")
    position = lax.axis_index("ctx")
    key_start = position * shard
    everyone = lax.all_gather(queries, "ctx", axis=0, tiled=True)
    blocks = everyone.reshape(ctx_count, shard, head_size)

    def attend(block, index):
        return partial_attention(block, index * shard, keys, values, key_start)

    def per_block(entry):
        block, index = entry
        return attend(block, index)

    outs, log_totals = lax.map(per_block, (blocks, jnp.arange(ctx_count, dtype=jnp.int32)))
    got_outs, got_totals = (
        lax.all_to_all(outs, "ctx", split_axis=0, concat_axis=0, tiled=True),
        lax.all_to_all(log_totals, "ctx", split_axis=0, concat_axis=0, tiled=True),
    )
    attended = merge_partials(got_outs, got_totals)
    tok_rows = stream_in.shape[0]
    width = stream_in.shape[1]
    chosen = attended
    term = jnp.dot(chosen, w_out, preferred_element_type=jnp.float32).astype(jnp.bfloat16)
    projected = lax.psum_scatter(
        lax.optimization_barrier(term).astype(jnp.float32).astype(jnp.bfloat16),
        "exp",
        scatter_dimension=0,
        tiled=True,
    ).astype(jnp.float32)
    hidden = stream_in.astype(jnp.float32) + projected
    normed = (
        hidden
        * lax.rsqrt(jnp.mean(hidden * hidden, axis=1, keepdims=True) + 1e-06)
        * norm_gain[None, :]
    ).astype(jnp.bfloat16)
    exp_count = lax.axis_size("exp")
    groups = ctx_count // PIECES
    expert_total = exp_count * groups
    routes_per = expert_ids.shape[1]
    capacity = min(tok_rows, max(2, 4 * routes_per * tok_rows // (3 * expert_total)))
    flat_ids = expert_ids.reshape(-1)
    one_hot = (flat_ids[:, None] == jnp.arange(expert_total, dtype=jnp.int32)[None, :]).astype(
        jnp.int32
    )
    ranking = jnp.sum((jnp.cumsum(one_hot, axis=0) - one_hot) * one_hot, axis=1)
    slot_index = flat_ids * capacity + ranking
    placing = (
        slot_index[None, :] == jnp.arange(expert_total * capacity, dtype=jnp.int32)[:, None]
    ).astype(jnp.bfloat16)
    place_tokens = jnp.sum(placing.reshape(expert_total * capacity, tok_rows, routes_per), axis=2)
    outgoing = jnp.dot(place_tokens, normed, preferred_element_type=jnp.float32).astype(
        jnp.bfloat16
    )
    outgoing = outgoing.reshape(groups, exp_count, capacity, width)
    gate_local = w_gate[0, 0]
    up_local = w_up[0, 0]
    down_local = w_down[0, 0]
    arrived = lax.all_to_all(outgoing, "exp", split_axis=1, concat_axis=1, tiled=True)
    copies = jnp.repeat(arrived, PIECES, axis=0)
    mine = lax.all_to_all(copies, "ctx", split_axis=0, concat_axis=0, tiled=True)
    chosen = mine.reshape(-1, width)
    gate_value = lax.dot_general(
        chosen, gate_local, (((1,), (1,)), ((), ())), preferred_element_type=jnp.float32
    )
    up_value = lax.dot_general(
        chosen, up_local, (((1,), (1,)), ((), ())), preferred_element_type=jnp.float32
    )
    activated = (jax.nn.silu(gate_value) * up_value).astype(jnp.bfloat16)
    down = jnp.dot(activated, down_local, preferred_element_type=jnp.float32).astype(jnp.bfloat16)
    pieces = down.reshape(mine.shape)
    back = lax.all_to_all(pieces, "ctx", split_axis=0, concat_axis=0, tiled=True)
    summed = jnp.sum(
        back.reshape(groups, PIECES, exp_count, capacity, width).astype(jnp.float32), axis=1
    ).astype(jnp.bfloat16)
    returning = lax.all_to_all(summed, "exp", split_axis=1, concat_axis=1, tiled=True)
    gathered = lax.dot_general(
        placing,
        returning.reshape(expert_total * capacity, width),
        (((0,), (0,)), ((), ())),
        preferred_element_type=jnp.float32,
    )
    gathered = gathered.reshape(tok_rows, routes_per, width)
    combined = jnp.sum(gates[:, :, None] * gathered, axis=1)
    return (hidden + combined).astype(jnp.bfloat16)


def solution(mesh):
    placed = (
        P(("ctx", "exp"), None),
        P("ctx", "exp"),
        P("ctx", "exp"),
        P("ctx", "exp"),
        P("exp", None),
        P(),
        P(("ctx", "exp"), None),
        P(("ctx", "exp"), None),
        P("ctx", "exp", None, None),
        P("ctx", "exp", None, None),
        P("ctx", "exp", None, None),
    )
    return jax.shard_map(
        on_device, mesh=mesh, in_specs=placed, out_specs=P(("ctx", "exp"), None), check_vma=False
    )
```

profile of v0, /device:TPU:3, one launch (start us, length us, event | category | flops | bytes accessed | tf_op | source)
XLA Modules:
  0.0 483.3 jit_solution(12921288830665762225)
XLA Ops:
  6.5 29.3 %all_gather.3 = bf16[2048,128]{1,0:T(8,128)(2,1)S(1)} all-gather(bf16[256,128]{1,0:T(8,128)(2,1)} %param.14), channel_id=1, replica_groups=mesh['ctx'=8,'exp'=32] {'ctx'}, dimensions={0}, use_global_device_ids=true | all-gather | bytes 589824 | tf_op jit(solution)/shard_map/all_gather | solution.py:49
  35.8 35.0 %while.12 = (s32[]{:T(128)}, f32[8,256,128]{2,1,0:T(8,128)}, f32[8,256]{1,0:T(8,128)S(1)}, s32[]{:T(128)}, s32[8]{0:T(128)S(1)}, /*index=5*/bf16[8,256,128]{2,1,...) while((s32[]{:T(128)}, f32[8,256,128]{2,1,0:T(8,128)}, ...), condition=%wide.region_4.5_spmd, body=%wide.region_0.4_spmd.sunk | while | flops 34538752 | bytes 1140373 | solution.py:59
  38.3 1.8 fusion.60
  42.7 1.8 fusion.60
  47.1 1.8 fusion.60
  51.4 1.8 fusion.60
  55.8 1.8 fusion.60
  64.6 1.8 fusion.60
  68.9 1.8 fusion.60
  70.8 11.9 %all_to_all.37 = f32[8,1,256]{2,1,0:T(1,128)S(1)} all-to-all(f32[8,1,256]{2,1,0:T(1,128)S(1)} %all_to_all.24), channel_id=1, replica_groups=mesh['ctx'=8,'exp'=32] {'ctx'}, dimensions={0} | all-to-all | bytes 16384 | tf_op jit(solution)/shard_map/all_to_all | solution.py:62
  82.8 4.4 all-to-all-start
  87.3 11.0 %all-to-all-done = f32[8,256,128]{2,1,0:T(8,128)} async-done(((f32[8,256,128]{2,1,0:T(8,128)}), f32[8,256,128]{2,1,0:T(8,128)}, u32[]{:S(2)}, u32[]{:S(2)}) %all-to-all-start) | async-done | bytes 1048608 | tf_op jit(solution)/shard_map/all_to_all | solution.py:61
  99.9 3.3 convolution_convert_fusion.1
  103.9 119.2 %reduce-scatter.2.cloned.1.call-done = bf16[8,4096]{1,0:T(8,128)(2,1)} async-done(((bf16[256,4096]{1,0:T(8,128)(2,1)}), bf16[8,4096]{1,0:T(8,128)(2,1)}) %reduce-scatter.2.cloned.1.call-update) | async-done | bytes 65552 | tf_op jit(solution)/shard_map/reduce_scatter | solution.py:69
  224.1 2.3 convolution_convert_fusion.2
  226.4 2.5 reshape.152
  228.9 2.1 copy.28
  231.1 40.5 %all_to_all.38 = bf16[2,32,2,4096]{3,2,0,1:T(2,128)(2,1)S(1)} all-to-all(bf16[2,32,2,4096]{3,2,0,1:T(2,128)(2,1)S(1)} %copy.28), channel_id=1, replica_groups=mesh['ctx'=8,'exp'=32] {'exp'}, dimensions={1} | all-to-all | bytes 2097152 | tf_op jit(solution)/shard_map/all_to_all | solution.py:103
  271.5 1.9 copy.29
  273.4 7.7 %broadcast_in_dim.51 = bf16[2,4,32,2,4096]{4,3,2,1,0:T(2,128)(2,1)} broadcast(bf16[2,32,2,4096]{3,2,1,0:T(2,128)(2,1)} %copy.29), dimensions={0,2,3,4} | broadcast | bytes 5242880 | tf_op jit(solution)/shard_map/broadcast_in_dim | solution.py:104
  281.1 55.2 %all_to_all.39 = bf16[8,32,2,4096]{3,2,1,0:T(2,128)(2,1)} all-to-all(bf16[8,32,2,4096]{3,2,1,0:T(2,128)(2,1)} %bitcast.64), channel_id=1, replica_groups=mesh['ctx'=8,'exp'=32] {'ctx'}, dimensions={0} | all-to-all | bytes 8388608 | tf_op jit(solution)/shard_map/all_to_all | solution.py:105
  336.3 7.2 %reshape.154 = bf16[512,4096]{1,0:T(8,128)(2,1)} reshape(bf16[8,32,2,4096]{3,2,1,0:T(2,128)(2,1)} %all_to_all.39) | data formatting | bytes 8388608 | tf_op jit(solution)/shard_map/reshape | solution.py:106
  343.5 5.7 %fusion.17 = f32[512,352]{0,1:T(8,128)} fusion(bf16[512,4096]{1,0:T(8,128)(2,1)} %reshape.154, bf16[1,1,352,4096]{3,2,1,0:T(8,128)(2,1)} %param.21), kind=kOutput, calls=%fused_computation.34 | convolution fusion | flops 1476395008 | bytes 7798784 | tf_op jit(solution)/shard_map/dot_general | solution.py:107
  349.2 9.2 %convolution_convert_fusion = bf16[512,4096]{1,0:T(8,128)(2,1)} fusion(bf16[1,1,352,4096]{3,2,1,0:T(8,128)(2,1)S(1)} %copy-done, bf16[512,4096]{1,0:T(8,128)(2,1)} %reshape.154, bf16[1,1,352,4096]{3,2,1,0:T(8,128)(2,1)} %param.22, f32[512,352]{0,1:T(8,128)} %fusion.17), kind=kOutput, calls=%fused_computation.26 | convolution fusion | flops 2955968512 | bytes 14876672 | tf_op jit(solution)/shard_map/dot_general | solution.py:114
  358.4 7.6 %reshape.155 = bf16[8,32,2,4096]{3,2,1,0:T(2,128)(2,1)} reshape(bf16[512,4096]{1,0:T(8,128)(2,1)} %convolution_convert_fusion) | data formatting | bytes 8388608 | tf_op jit(solution)/shard_map/reshape | solution.py:115
  366.0 51.5 %all_to_all.40 = bf16[8,32,2,4096]{3,2,1,0:T(2,128)(2,1)} all-to-all(bf16[8,32,2,4096]{3,2,1,0:T(2,128)(2,1)} %reshape.155), channel_id=1, replica_groups=mesh['ctx'=8,'exp'=32] {'ctx'}, dimensions={0} | all-to-all | bytes 8388608 | tf_op jit(solution)/shard_map/all_to_all | solution.py:116
  417.5 9.2 %bitcast_reduce_fusion = bf16[2,32,2,4096]{3,2,1,0:T(2,128)(2,1)} fusion(bf16[8,32,2,4096]{3,2,1,0:T(2,128)(2,1)} %all_to_all.40), kind=kLoop, calls=%fused_computation.30 | loop fusion | flops 1572864 | bytes 5242880 | tf_op jit(solution)/shard_map/reduce_sum | solution.py:117
  426.8 3.4 copy.30
  430.2 10.2 %all-to-all-start.5 = ((bf16[2,32,2,4096]{3,2,0,1:T(2,128)(2,1)}), bf16[2,32,2,4096]{3,2,0,1:T(2,128)(2,1)}, u32[]{:S(2)}, u32[]{:S(2)}) async-start(bf16[2,32,2,4096]{3,2,0,1:T(2,128)(2,1)} %copy.30), calls=%async_computation.6 | async-start | bytes 2097152 | tf_op jit(solution)/shard_map/all_to_all | solution.py:120
  440.5 28.2 %all-to-all-done.5 = bf16[2,32,2,4096]{3,2,0,1:T(2,128)(2,1)} async-done(((bf16[2,32,2,4096]{3,2,0,1:T(2,128)(2,1)}), bf16[2,32,2,4096]{3,2,0,1:T(2,128)(2,1)}, u32[]{:S(2)}, u32[]{:S(2)}) %all-to-all-start.5) | async-done | bytes 1048608 | tf_op jit(solution)/shard_map/all_to_all | solution.py:120
  468.7 3.3 copy.31
  471.9 2.3 reshape.158
  (108 shorter events, 23.2 us)
Async XLA Ops:
  6.5 342.7 %copy-start = (bf16[1,1,352,4096]{3,2,1,0:T(8,128)(2,1)S(1)}, bf16[1,1,352,4096]{3,2,1,0:T(8,128)(2,1)}, u32[]{:S(2)}) copy-start(bf16[1,1,352,4096]{3,2,1,0:T(8,128)(2,1)} %param.23) | copy-start | bytes 8650756
  82.8 20.4 %copy-start.4 = (s32[8,6]{1,0:T(8,128)S(1)}, s32[8,6]{1,0:T(8,128)}, u32[]{:S(2)}) copy-start(s32[8,6]{1,0:T(8,128)} %param.19) | copy-start | bytes 580
  82.8 140.3 %copy-start.1 = (bf16[8,4096]{1,0:T(8,128)(2,1)S(1)}, bf16[8,4096]{1,0:T(8,128)(2,1)}, u32[]{:S(2)}) copy-start(bf16[8,4096]{1,0:T(8,128)(2,1)} %param.13) | copy-start | bytes 196612
  82.8 141.3 %copy-start.3 = (f32[4096]{0:T(1024)S(1)}, f32[4096]{0:T(1024)}, u32[]{:S(2)}) copy-start(f32[4096]{0:T(1024)} %param.18) | copy-start | bytes 49156
  82.8 15.5 %all-to-all-start = ((f32[8,256,128]{2,1,0:T(8,128)}), f32[8,256,128]{2,1,0:T(8,128)}, u32[]{:S(2)}, u32[]{:S(2)}) async-start(f32[8,256,128]{2,1,0:T(8,128)} %get-tuple-element.48), calls=%async_computation | async-start | bytes 2097152 | tf_op jit(solution)/shard_map/all_to_all | solution.py:61
  87.2 135.9 %reduce-scatter.2.cloned.1.call-start = ((), (), s32[]{:S(2)}) async-start(), calls=%async_computation.7 | async-start | bytes 2162688 | tf_op jit(solution)/shard_map/reduce_scatter | solution.py:69
  417.5 22.9 %copy-start.5 = (f32[8,6]{1,0:T(8,128)S(1)}, f32[8,6]{1,0:T(8,128)}, u32[]{:S(2)}) copy-start(f32[8,6]{1,0:T(8,128)} %param.20) | copy-start | bytes 580
  430.2 45.6 %copy-start.2 = (bf16[8,4096]{1,0:T(8,128)(2,1)S(1)}, bf16[8,4096]{1,0:T(8,128)(2,1)}, u32[]{:S(2)}) copy-start(bf16[8,4096]{1,0:T(8,128)(2,1)} %reduce-scatter.2.cloned.1.call-done) | copy-start | bytes 196612
  430.2 38.5 %all-to-all-start.5 = ((bf16[2,32,2,4096]{3,2,0,1:T(2,128)(2,1)}), bf16[2,32,2,4096]{3,2,0,1:T(2,128)(2,1)}, u32[]{:S(2)}, u32[]{:S(2)}) async-start(bf16[2,32,2,4096]{3,2,0,1:T(2,128)(2,1)} %copy.30), calls=%async_computation.6 | async-start | bytes 2097152 | tf_op jit(solution)/shard_map/all_to_all | solution.py:120
Sparse Core Ops, SparseCore 0:
  103.3 119.7 reduce-scatter.1
where the time goes:
time: 486 us; the launch traced here: 483 us
  blocking collectives  188 us (39%)
  waiting for transfers between devices  158 us (33%)
  matrix products  45 us (9%)
  local copies, waits for them, and re-layouts  43.4 us (9%)
  other arithmetic  15.1 us (3%)
  starting transfers between devices  14.6 us (3%)
  between operations  13.5 us (3%)
  loops' own time  4.86 us (1%)
    reduce_scatter x1, waiting for transfers between devices, on_device(): lax.psum_scatter(lax.optimization_barrier(term).astype(jnp.float32).astyp...  119 us
    all_to_all x1, blocking collectives, on_device(): lax.all_to_all(copies, 'ctx', split_axis=0, concat_axis=0, tiled=True)  55.2 us
    all_to_all x1, blocking collectives, on_device(): lax.all_to_all(pieces, 'ctx', split_axis=0, concat_axis=0, tiled=True)  51.5 us
    all_to_all x1, blocking collectives, on_device(): lax.all_to_all(outgoing, 'exp', split_axis=1, concat_axis=1, tiled=True)  40.5 us
    all_gather x1, blocking collectives, on_device(): everyone = lax.all_gather(queries, 'ctx', axis=0, tiled=True)  29.3 us
    all_to_all x1, waiting for transfers between devices, on_device(): lax.all_to_all(summed, 'exp', split_axis=1, concat_axis=1, tiled=True)  28.2 us
    dot_general x8, matrix products, partial_attention(): jnp.dot(probs, value_block, preferred_element_type=jnp.float32)  14.5 us
    all_to_all x1, blocking collectives, on_device(): lax.all_to_all(log_totals, 'ctx', split_axis=0, concat_axis=0, tiled=True)  11.9 us
  transfers between devices with their start and end apart: 3, of which 3 were waited for; matrix products, arithmetic and copies ran while one was open for 0% of the time, Pallas kernels for 0%

commit v1 on v0

v1 whole, which is shorter than its diff:
```python
import jax
import jax.numpy as jnp
from jax import lax
from jax.experimental import pallas as pl
from jax.experimental.pallas import tpu as pltpu
from jax.sharding import Mesh, PartitionSpec as P

CTX = ("xh", "y")
QUAD = ("xl", "core")
EXP = ("z", "xl", "core")
HOME = ("xh", "z", "xl", "core")

SUB = 16
LANE = 256

f32 = jnp.float32
bf16 = jnp.bfloat16
VMEM = pl.BlockSpec(memory_space=pltpu.VMEM)
SMEM = pl.BlockSpec(memory_space=pltpu.SMEM)


def swap_matrix(outer, inner):
    size = outer * inner
    row = lax.broadcasted_iota(jnp.int32, (size, size), 0)
    col = lax.broadcasted_iota(jnp.int32, (size, size), 1)
    return (col == (row % inner) * outer + row // inner).astype(bf16)


def attention_kernel(index, q_ref, kv_ref, out_ref):
    own = index[0]
    q = q_ref[...]
    head = q.shape[1]
    scale = head ** (-0.5)

    def scores_of(j):
        return (
            lax.dot_general(
                q, kv_ref[j, :, :head], (((1,), (1,)), ((), ())), preferred_element_type=f32
            )
            * scale
        )

    scores = scores_of(own)
    row = lax.broadcasted_iota(jnp.int32, scores.shape, 0)
    col = lax.broadcasted_iota(jnp.int32, scores.shape, 1)
    scores = jnp.where(col <= row, scores, -1e30)
    top = jnp.max(scores, axis=1, keepdims=True)
    weights = jnp.exp(scores - top)
    total = jnp.sum(weights, axis=1, keepdims=True)
    acc = jnp.dot(weights.astype(bf16), kv_ref[own, :, head:], preferred_element_type=f32)

    def step(j, carry):
        top, total, acc = carry
        scores = scores_of(j)
        higher = jnp.maximum(top, jnp.max(scores, axis=1, keepdims=True))
        fade = jnp.exp(top - higher)
        weights = jnp.exp(scores - higher)
        total = total * fade + jnp.sum(weights, axis=1, keepdims=True)
        acc = acc * fade + jnp.dot(
            weights.astype(bf16), kv_ref[j, :, head:], preferred_element_type=f32
        )
        return higher, total, acc

    top, total, acc = lax.fori_loop(0, own, step, (top, total, acc))
    out_ref[...] = (acc / total).astype(bf16)


def project_kernel(a0, a1, a2, a3, w0, w1, w2, w3, out_ref):
    acc = jnp.dot(a0[...], w0[...], preferred_element_type=f32)
    for a, w in ((a1, w1), (a2, w2), (a3, w3)):
        acc += jnp.dot(a[...], w[...], preferred_element_type=f32)
    out_ref[...] = acc.astype(bf16)


def dispatch_kernel(ids, proj, stream, gain, hidden, first, second, count, rows):
    tokens, width = stream.shape
    parts = proj.shape[0]
    part = width // parts
    squares = jnp.zeros((tokens, 1), f32)
    for p in range(parts):
        cols = slice(p * part, (p + 1) * part)
        h = stream[:, cols].astype(f32) + proj[p]
        hidden[:, cols] = h
        squares += jnp.sum(h * h, axis=1, keepdims=True)
    norm = lax.rsqrt(squares / width + 1e-06)
    blocks = []
    for k in range(SUB):
        cols = slice(k * LANE, (k + 1) * LANE)
        blocks.append(hidden[:, cols] * norm * gain[:, cols])
    normed = jnp.concatenate(blocks, axis=0).astype(bf16)
    swapped = jnp.dot(swap_matrix(tokens, SUB), normed, preferred_element_type=f32)
    rows[...] = swapped.astype(bf16).reshape(rows.shape)
    first[...] = jnp.zeros_like(first)
    second[...] = jnp.zeros_like(second)
    for e in range(first.shape[0]):
        count[e] = 0
    for t in range(tokens):
        for k in range(ids.shape[1]):
            e = ids[t, k]
            seen = count[e]
            count[e] = seen + 1

            @pl.when(seen == 0)
            def _():
                first[e] = rows[t]

            @pl.when(seen != 0)
            def _():
                second[e] = rows[t]


def expert_kernel(x0, x1, x2, x3, gate_ref, up_ref, down_ref, o0, o1, o2, o3, flat, mixed):
    swap = swap_matrix(SUB, SUB)
    per = x0.shape[0] // SUB
    for s, x in enumerate((x0, x1, x2, x3)):
        for b in range(per):
            block = x[b * SUB : (b + 1) * SUB].reshape(SUB * SUB, LANE)
            turned = jnp.dot(swap, block, preferred_element_type=f32).astype(bf16)
            at = (s * per + b) * SUB
            for k in range(SUB):
                flat[at : at + SUB, k * LANE : (k + 1) * LANE] = turned[k * SUB : (k + 1) * SUB]
    x = flat[...]
    gate = lax.dot_general(x, gate_ref[...], (((1,), (1,)), ((), ())), preferred_element_type=f32)
    up = lax.dot_general(x, up_ref[...], (((1,), (1,)), ((), ())), preferred_element_type=f32)
    activated = (gate / (1.0 + jnp.exp(-gate)) * up).astype(bf16)
    for k in range(SUB):
        down = jnp.dot(
            activated, down_ref[:, k * LANE : (k + 1) * LANE], preferred_element_type=f32
        ).astype(bf16)
        for g in range(4 * per):
            mixed[g, k * SUB : (k + 1) * SUB, :] = down[g * SUB : (g + 1) * SUB]
    for s, o in enumerate((o0, o1, o2, o3)):
        for b in range(per):
            turned = jnp.dot(swap, mixed[s * per + b], preferred_element_type=f32).astype(bf16)
            o[b * SUB : (b + 1) * SUB] = turned.reshape(SUB, SUB, LANE)


def combine_kernel(ids, gates, hidden, first, second, out_ref, count, total):
    tokens = hidden.shape[0]
    for e in range(first.shape[0]):
        count[e] = 0
    for t in range(tokens):
        acc = jnp.zeros((SUB, LANE), f32)
        for k in range(ids.shape[1]):
            e = ids[t, k]
            seen = count[e]
            count[e] = seen + 1
            routed = jnp.where(seen == 0, first[e].astype(f32), second[e].astype(f32))
            acc += gates[t, k] * routed
        for k in range(SUB):
            total[t : t + 1, k * LANE : (k + 1) * LANE] = acc[k : k + 1]
    out_ref[...] = (hidden[...] + total[...]).astype(bf16)


def shift(steps, count):
    return [(i, (i + steps) % count) for i in range(count)]


def flip(bits):
    return [(i, i ^ bits) for i in range(4)]


def on_device(
    stream_in, queries, keys, values, w_out, norm_gain, expert_ids, gates, w_gate, w_up, w_down
):
    shard, head = queries.shape
    tokens, width = stream_in.shape
    n_ctx = 8
    n_z = 8
    experts = 64
    quarter = width // 4
    place = lax.axis_index("xh") * 4 + lax.axis_index("y")
    quad = lax.axis_index(QUAD)

    weights = []
    for d in range(4):
        cols = lax.dynamic_slice_in_dim(w_out, (quad ^ d) * quarter, quarter, 1)
        weights.append(cols if d == 0 else lax.ppermute(cols, QUAD, flip(d)))

    both = jnp.concatenate([keys, values], axis=1)
    copies = jnp.broadcast_to(both[None], (n_ctx, shard, 2 * head))
    everyone = lax.all_to_all(copies, CTX, 0, 0, tiled=True)
    attended = pl.pallas_call(
        attention_kernel,
        out_shape=jax.ShapeDtypeStruct((shard, head), bf16),
        in_specs=[SMEM, VMEM, VMEM],
        out_specs=VMEM,
        name="attention",
    )(place.reshape(1).astype(jnp.int32), queries, everyone)

    heads = [attended] + [lax.ppermute(attended, QUAD, flip(d)) for d in (1, 2, 3)]
    term = pl.pallas_call(
        project_kernel,
        out_shape=jax.ShapeDtypeStruct((shard, quarter), bf16),
        in_specs=[VMEM] * 8,
        out_specs=VMEM,
        name="project",
    )(*heads, *weights)
    terms = lax.all_to_all(term.reshape(n_z, shard // n_z, quarter), "z", 0, 0, tiled=True)
    summed = jnp.sum(terms.astype(f32), axis=0)
    proj = lax.all_to_all(summed.reshape(4, tokens, quarter), QUAD, 0, 0, tiled=True)

    row_block = (experts, SUB, LANE)
    hidden, first, second = pl.pallas_call(
        dispatch_kernel,
        out_shape=(
            jax.ShapeDtypeStruct((tokens, width), f32),
            jax.ShapeDtypeStruct(row_block, bf16),
            jax.ShapeDtypeStruct(row_block, bf16),
        ),
        in_specs=[SMEM, VMEM, VMEM, VMEM],
        out_specs=(VMEM, VMEM, VMEM),
        scratch_shapes=[
            pltpu.SMEM((experts,), jnp.int32),
            pltpu.VMEM((tokens, SUB, LANE), bf16),
        ],
        name="dispatch",
    )(expert_ids, proj, stream_in, norm_gain.reshape(1, width))

    expert_call = pl.pallas_call(
        expert_kernel,
        out_shape=(jax.ShapeDtypeStruct(row_block, bf16),) * 4,
        in_specs=[VMEM] * 7,
        out_specs=(VMEM,) * 4,
        scratch_shapes=[
            pltpu.VMEM((4 * experts, width), bf16),
            pltpu.VMEM((4 * experts // SUB, SUB * SUB, LANE), bf16),
        ],
        compiler_params=pltpu.CompilerParams(vmem_limit_bytes=40 * 1024 * 1024),
        name="experts",
    )
    returned = []
    for rows in (first, second):
        own = lax.all_to_all(rows, HOME, 0, 0, tiled=True)
        others = [lax.ppermute(own, "y", shift(d, 4)) for d in (1, 2, 3)]
        outs = expert_call(own, *others, w_gate[0, 0], w_up[0, 0], w_down[0, 0])
        pieces = [outs[0]] + [lax.ppermute(outs[d], "y", shift(-d, 4)) for d in (1, 2, 3)]
        total = pieces[0].astype(f32)
        for piece in pieces[1:]:
            total = total + piece.astype(f32)
        returned.append(lax.all_to_all(total.astype(bf16), HOME, 0, 0, tiled=True))

    return pl.pallas_call(
        combine_kernel,
        out_shape=jax.ShapeDtypeStruct((tokens, width), bf16),
        in_specs=[SMEM, SMEM, VMEM, VMEM, VMEM],
        out_specs=VMEM,
        scratch_shapes=[pltpu.SMEM((experts,), jnp.int32), pltpu.VMEM((tokens, width), f32)],
        name="combine",
    )(expert_ids, gates, hidden, *returned)


def solution(mesh):
    fine = Mesh(mesh.devices.reshape(2, 4, 8, 2, 2), ("xh", "y", "z", "xl", "core"))
    token = CTX + EXP
    placed = (
        P(token, None),
        P(CTX, EXP),
        P(CTX, EXP),
        P(CTX, EXP),
        P(EXP, None),
        P(),
        P(token, None),
        P(token, None),
        P(CTX, EXP, None, None),
        P(CTX, EXP, None, None),
        P(CTX, EXP, None, None),
    )
    return jax.shard_map(
        on_device, mesh=fine, in_specs=placed, out_specs=P(token, None), check_vma=False
    )
```

time: 486 us -> 254 us (0.52)
  blocking collectives: 188 us -> 81.7 us
  waiting for transfers between devices: 158 us -> 96.8 us
  matrix products: 45 us -> 0 us
  local copies, waits for them, and re-layouts: 43.4 us -> 11.7 us
  Pallas kernels: 0 us -> 23.5 us
  starting transfers between devices: 14.6 us -> 34.5 us
  between operations: 13.5 us -> 0.14 us
  other arithmetic: 15.1 us -> 3.93 us
  loops' own time: 4.86 us -> 0 us
    reduce_scatter x1 -> x0, waiting for transfers between devices: 119 us -> none  [on_device(): lax.psum_scatter(lax.optimization_barrier(term).astype(jnp.float32).astyp...]
    ppermute x0 -> x18, waiting for transfers between devices: none -> 85.7 us  [the longest x6 48.6 us: on_device(): lax.ppermute(outs[d], 'y', shift(-d, 4))]
    all_to_all x4, blocking collectives: 159 us -> 81.7 us  [the longest x1 25.7 us: on_device(): own = lax.all_to_all(rows, HOME, 0, 0, tiled=True)]
    dot_general x21 -> x0, matrix products: 45 us -> none  [the longest x8 14.5 us: partial_attention(): jnp.dot(probs, value_block, preferred_element_type=jnp.float32)]
    all_gather x1 -> x0, blocking collectives: 29.3 us -> none  [on_device(): everyone = lax.all_gather(queries, 'ctx', axis=0, tiled=True)]
    all_to_all x2 -> x3, waiting for transfers between devices: 39.2 us -> 11.2 us  [the longest x1 11.2 us: on_device(): everyone = lax.all_to_all(copies, CTX, 0, 0, tiled=True)]
    pallas_call x0 -> x6, Pallas kernels: none -> 23.5 us  [the longest x2 13.1 us: on_device(): outs = expert_call(own, *others, w_gate[0, 0], w_up[0, 0], w_down[0, 0])]
    reshape x6 -> x0, local copies, waits for them, and re-layouts: 21.8 us -> none  [the longest x1 7.62 us: on_device(): pieces = down.reshape(mine.shape)]
  transfers between devices with their start and end apart: 3 -> 21, of which waited for: 3 -> 13; matrix products, arithmetic and copies ran while one was open for 0% -> 1% of each run, Pallas kernels for 0% -> 6%
where the time goes in v1:
time: 254 us; the launch traced here: 252 us
  waiting for transfers between devices  96.8 us (38%)
  blocking collectives  81.7 us (32%)
  starting transfers between devices  34.5 us (14%)
  Pallas kernels  23.5 us (9%)
  local copies, waits for them, and re-layouts  11.7 us (5%)
  other arithmetic  3.93 us (2%)
    ppermute x6, waiting for transfers between devices, on_device(): lax.ppermute(outs[d], 'y', shift(-d, 4))  48.6 us
    ppermute x6, waiting for transfers between devices, on_device(): others = [lax.ppermute(own, 'y', shift(d, 4)) for d in (1, 2, 3)]  32.6 us
    all_to_all x1, blocking collectives, on_device(): own = lax.all_to_all(rows, HOME, 0, 0, tiled=True)  25.7 us
    all_to_all x1, blocking collectives, on_device(): lax.all_to_all(term.reshape(n_z, shard // n_z, quarter), 'z', 0, 0, tiled...  23.3 us
    all_to_all x1, blocking collectives, on_device(): returned.append(lax.all_to_all(total.astype(bf16), HOME, 0, 0, tiled=True))  23 us
    pallas_call x2, Pallas kernels, on_device(): outs = expert_call(own, *others, w_gate[0, 0], w_up[0, 0], w_down[0, 0])  13.1 us
    all_to_all x1, waiting for transfers between devices, on_device(): everyone = lax.all_to_all(copies, CTX, 0, 0, tiled=True)  11.2 us
    all_to_all x1, blocking collectives, on_device(): lax.all_to_all(summed.reshape(4, tokens, quarter), QUAD, 0, 0, tiled=True)  9.76 us
  transfers between devices with their start and end apart: 21, of which 13 were waited for; matrix products, arithmetic and copies ran while one was open for 1% of the time, Pallas kernels for 6%

profile of v1, /device:TPU:3, one launch (start us, length us, event | category | flops | bytes accessed | tf_op | source)
XLA Modules:
  0.0 252.3 jit_solution(5075027660998841879)
XLA Ops:
  2.0 5.8 %all-to-all-start = ((bf16[8,256,256]{2,1,0:T(8,128)(2,1)}), bf16[8,256,256]{2,1,0:T(8,128)(2,1)S(1)}, u32[]{:S(2)}, u32[]{:S(2)}) async-start(bf16[8,256,256]{2,1,0:T(8,128)(2,1)} %broadcast_in_dim.2), calls=%async_computation | async-start | bytes 2097152 | tf_op jit(solution)/shard_map/all_to_all | solution.py:182
  8.7 2.0 collective-permute-start.5
  11.0 11.2 %all-to-all-done.kv_ref = bf16[8,256,256]{2,1,0:T(8,128)(2,1)S(1)} async-done(((bf16[8,256,256]{2,1,0:T(8,128)(2,1)}), bf16[8,256,256]{2,1,0:T(8,128)(2,1)S(1)}, u32[]{:S(2)}, u32[]{:S(2)}) %all-to-all-start) | async-done | bytes 1048608 | tf_op jit(solution)/shard_map/all_to_all | solution.py:182
  23.1 2.3 attention.1.a0
  25.5 4.2 %collective-permute-start.2 = (bf16[256,128]{1,0:T(8,128)(2,1)}, bf16[256,128]{1,0:T(8,128)(2,1)S(1)}, u32[]{:S(2)}, u32[]{:S(2)}) collective-permute-start(bf16[256,128]{1,0:T(8,128)(2,1)} %attention.1.a0), channel_id=1, source_target_pairs={{0,3},{1,2},{2,1},{3,0},{4,7},{5,6},{6,5},{7,4},{8,11},{9,10},{10,... | collective-permute-start | bytes 196616 | tf_op jit(solution)/shard_map/ppermute | solution.py:191
  30.2 1.5 collective-permute-done.4.w2
  31.7 3.0 %collective-permute-done.2.a3 = bf16[256,128]{1,0:T(8,128)(2,1)S(1)} collective-permute-done((bf16[256,128]{1,0:T(8,128)(2,1)}, bf16[256,128]{1,0:T(8,128)(2,1)S(1)}, u32[]{:S(2)}, u32[]{:S(2)}) %collective-permute-start.2) | collective-permute-done | bytes 65568 | tf_op jit(solution)/shard_map/ppermute | solution.py:191
  35.4 2.9 %project.1 = bf16[256,1024]{1,0:T(8,128)(2,1)} custom-call(bf16[256,128]{1,0:T(8,128)(2,1)} %attention.1.a0, bf16[256,128]{1,0:T(8,128)(2,1)} %copy-done.13, bf16[256,128]{1,0:T(8,128)(2,1)} %copy-done.12, bf16[256,128]{1,0:T(8,128)(2,1)} %copy-done.11, bf16[128,1024]{1,0:T(8,128)(2,1)} %get-tuple-element.29.w0, bf16[128,1024]{1,0:T(8,128)(2,1)} %copy-done.9, ...), custom_call_target="tpu_custom_call" | custom-call | tf_op jit(solution)/shard_map/project/pallas_call | solution.py:192
  38.3 23.3 %all_to_all.35 = bf16[8,32,1024]{2,1,0:T(8,128)(2,1)S(1)} all-to-all(bf16[8,32,1024]{2,1,0:T(8,128)(2,1)} %bitcast.13), channel_id=1, replica_groups=mesh['xh'=2,'y'=4,'z'=8,'xl'=2,'core'=2] {'z'}, dimensions={0} | all-to-all | bytes 1048576 | tf_op jit(solution)/shard_map/all_to_all | solution.py:199
  61.7 9.8 %all_to_all.36.proj = f32[4,8,1024]{2,1,0:T(8,128)} all-to-all(f32[4,8,1024]{2,1,0:T(8,128)S(1)} %bitcast.14), channel_id=1, replica_groups=mesh['xh'=2,'y'=4,'z'=8,'xl'=2,'core'=2] {'xl','core'}, dimensions={0} | all-to-all | bytes 262144 | tf_op jit(solution)/shard_map/all_to_all | solution.py:201
  71.5 2.9 %dispatch.1 = (f32[8,4096]{1,0:T(8,128)}, bf16[64,16,256]{2,1,0:T(8,128)(2,1)}, bf16[64,16,256]{2,1,0:T(8,128)(2,1)}) custom-call(s32[8,6]{1,0:T(8,128)} %ids.3, f32[4,8,1024]{2,1,0:T(8,128)} %all_to_all.36.proj, bf16[8,4096]{1,0:T(8,128)(2,1)} %stream.1, f32[1,4096]{1,0:T(1,128)} %bitcast.15), custom_call_target="tpu_custom_call" | custom-call | tf_op jit(solution)/shard_map/dispatch/pallas_call | solution.py:204
  74.4 25.7 %all_to_all.37.x0 = bf16[64,16,256]{2,1,0:T(8,128)(2,1)} all-to-all(bf16[64,16,256]{2,1,0:T(8,128)(2,1)} %get-tuple-element.22), channel_id=1, replica_groups=mesh['xh'=2,'y'=4,'z'=8,'xl'=2,'core'=2] {'xh','z','xl','core'}, dimensions={0} | all-to-all | bytes 1048576 | tf_op jit(solution)/shard_map/all_to_all | solution.py:234
  100.0 2.5 collective-permute-start.14
  103.7 6.1 %all-to-all-start.3 = ((bf16[64,16,256]{2,1,0:T(8,128)(2,1)}), bf16[64,16,256]{2,1,0:T(8,128)(2,1)S(1)}, u32[]{:S(2)}, u32[]{:S(2)}) async-start(bf16[64,16,256]{2,1,0:T(8,128)(2,1)} %get-tuple-element.17), calls=%async_computation.3 | async-start | bytes 1048576 | tf_op jit(solution)/shard_map/all_to_all | solution.py:234
  109.8 15.6 %collective-permute-done.14.x3 = bf16[64,16,256]{2,1,0:T(8,128)(2,1)} collective-permute-done((bf16[64,16,256]{2,1,0:T(8,128)(2,1)}, bf16[64,16,256]{2,1,0:T(8,128)(2,1)}, u32[]{:S(2)}, u32[]{:S(2)}) %collective-permute-start.14) | collective-permute-done | bytes 524320 | tf_op jit(solution)/shard_map/ppermute | solution.py:235
  125.4 4.1 %collective-permute-done.12.x1 = bf16[64,16,256]{2,1,0:T(8,128)(2,1)} collective-permute-done((bf16[64,16,256]{2,1,0:T(8,128)(2,1)}, bf16[64,16,256]{2,1,0:T(8,128)(2,1)}, u32[]{:S(2)}, u32[]{:S(2)}) %collective-permute-start.12) | collective-permute-done | bytes 524320 | tf_op jit(solution)/shard_map/ppermute | solution.py:235
  129.5 1.8 copy-done.1
  131.3 1.8 copy-done.3
  133.1 7.1 %experts.3 = (bf16[64,16,256]{2,1,0:T(8,128)(2,1)S(1)}, bf16[64,16,256]{2,1,0:T(8,128)(2,1)}, bf16[64,16,256]{2,1,0:T(8,128)(2,1)}, bf16[64,16,256]{2,1,0:T(8,128)(2,1)}) custom-call(bf16[64,16,256]{2,1,0:T(8,128)(2,1)} %all_to_all.37.x0, bf16[64,16,256]{2,1,0:T(8,128)(2,1)} %collective-permute-done.12.x1, bf16[64,16,256]{2,1,0:T(8,128)(2,1)} %collective-permute-done.13.x2, ...), custom_call_target="tpu_custom_call" | custom-call | tf_op jit(solution)/shard_map/experts/pallas_call | solution.py:236
  142.5 2.4 collective-permute-start.8
  146.1 8.3 %collective-permute-done.15 = bf16[64,16,256]{2,1,0:T(8,128)(2,1)} collective-permute-done((bf16[64,16,256]{2,1,0:T(8,128)(2,1)}, bf16[64,16,256]{2,1,0:T(8,128)(2,1)}, u32[]{:S(2)}, u32[]{:S(2)}) %collective-permute-start.15) | collective-permute-done | bytes 524320 | tf_op jit(solution)/shard_map/ppermute | solution.py:237
  155.2 14.2 %collective-permute-done.17 = bf16[64,16,256]{2,1,0:T(8,128)(2,1)} collective-permute-done((bf16[64,16,256]{2,1,0:T(8,128)(2,1)}, bf16[64,16,256]{2,1,0:T(8,128)(2,1)}, u32[]{:S(2)}, u32[]{:S(2)}) %collective-permute-start.17) | collective-permute-done | bytes 524320 | tf_op jit(solution)/shard_map/ppermute | solution.py:237
  169.4 2.6 %add_convert_fusion = bf16[64,16,256]{2,1,0:T(8,128)(2,1)} fusion(bf16[64,16,256]{2,1,0:T(8,128)(2,1)} %collective-permute-done.17, bf16[64,16,256]{2,1,0:T(8,128)(2,1)} %collective-permute-done.16, bf16[64,16,256]{2,1,0:T(8,128)(2,1)} %collective-permute-done.15, bf16[64,16,256]{2,1,0:T(8,128)(2,1)} %copy-done.5), kind=kLoop, calls=%fused_computation | loop fusion | flops 2097152 | bytes 2621440 | tf_op jit(solution)/shard_map/convert_element_type | solution.py:241
  172.0 5.4 %all-to-all-start.6 = ((bf16[64,16,256]{2,1,0:T(8,128)(2,1)}), bf16[64,16,256]{2,1,0:T(8,128)(2,1)}, u32[]{:S(2)}, u32[]{:S(2)}) async-start(bf16[64,16,256]{2,1,0:T(8,128)(2,1)} %add_convert_fusion), calls=%async_computation.6 | async-start | bytes 1048576 | tf_op jit(solution)/shard_map/all_to_all | solution.py:241
  177.7 12.5 %collective-permute-done.6.x1 = bf16[64,16,256]{2,1,0:T(8,128)(2,1)} collective-permute-done((bf16[64,16,256]{2,1,0:T(8,128)(2,1)S(1)}, bf16[64,16,256]{2,1,0:T(8,128)(2,1)}, u32[]{:S(2)}, u32[]{:S(2)}) %collective-permute-start.6) | collective-permute-done | bytes 524320 | tf_op jit(solution)/shard_map/ppermute | solution.py:235
  190.3 1.8 copy-done.2
  192.1 1.8 copy-done.4
  193.9 6.0 %experts.2 = (bf16[64,16,256]{2,1,0:T(8,128)(2,1)S(1)}, bf16[64,16,256]{2,1,0:T(8,128)(2,1)S(1)}, bf16[64,16,256]{2,1,0:T(8,128)(2,1)S(1)}, bf16[64,16,256]{2,1,0:T(8,128)(2,1)S(1)}) custom-call(bf16[64,16,256]{2,1,0:T(8,128)(2,1)S(1)} %all-to-all-done.3.x0, bf16[64,16,256]{2,1,0:T(8,128)(2,1)} %collective-permute-done.6.x1, ...), custom_call_target="tpu_custom_call" | custom-call | tf_op jit(solution)/shard_map/experts/pallas_call | solution.py:236
  201.5 11.4 %collective-permute-done.9 = bf16[64,16,256]{2,1,0:T(8,128)(2,1)S(1)} collective-permute-done((bf16[64,16,256]{2,1,0:T(8,128)(2,1)S(1)}, bf16[64,16,256]{2,1,0:T(8,128)(2,1)S(1)}, u32[]{:S(2)}, u32[]{:S(2)}) %collective-permute-start.9) | collective-permute-done | bytes 524320 | tf_op jit(solution)/shard_map/ppermute | solution.py:237
  213.6 13.2 %collective-permute-done.11 = bf16[64,16,256]{2,1,0:T(8,128)(2,1)S(1)} collective-permute-done((bf16[64,16,256]{2,1,0:T(8,128)(2,1)S(1)}, bf16[64,16,256]{2,1,0:T(8,128)(2,1)S(1)}, u32[]{:S(2)}, u32[]{:S(2)}) %collective-permute-start.11) | collective-permute-done | bytes 524320 | tf_op jit(solution)/shard_map/ppermute | solution.py:237
  227.1 23.0 %all_to_all.38.first = bf16[64,16,256]{2,1,0:T(8,128)(2,1)} all-to-all(bf16[64,16,256]{2,1,0:T(8,128)(2,1)S(1)} %add_convert_fusion.1), channel_id=1, replica_groups=mesh['xh'=2,'y'=4,'z'=8,'xl'=2,'core'=2] {'xh','z','xl','core'}, dimensions={0} | all-to-all | bytes 1048576 | tf_op jit(solution)/shard_map/all_to_all | solution.py:241
  250.1 2.2 combine.1
  (54 shorter events, 13.9 us)
Async XLA Ops:
  0.0 7.8 %copy-start.7 = (bf16[128,4096]{1,0:T(8,128)(2,1)S(1)}, bf16[128,4096]{1,0:T(8,128)(2,1)}, u32[]{:S(2)}) copy-start(bf16[128,4096]{1,0:T(8,128)(2,1)} %param.15) | copy-start | bytes 3145732
  2.0 20.1 %all-to-all-start = ((bf16[8,256,256]{2,1,0:T(8,128)(2,1)}), bf16[8,256,256]{2,1,0:T(8,128)(2,1)S(1)}, u32[]{:S(2)}, u32[]{:S(2)}) async-start(bf16[8,256,256]{2,1,0:T(8,128)(2,1)} %broadcast_in_dim.2), calls=%async_computation | async-start | bytes 2097152 | tf_op jit(solution)/shard_map/all_to_all | solution.py:182
  8.7 21.5 %collective-permute-start.5 = (bf16[128,1024]{1,0:T(8,128)(2,1)}, bf16[128,1024]{1,0:T(8,128)(2,1)S(1)}, u32[]{:S(2)}, u32[]{:S(2)}) collective-permute-start(bf16[128,1024]{1,0:T(8,128)(2,1)} %get-tuple-element.27), channel_id=1, source_target_pairs={{0,3},{1,2},{2,1},{3,0},{4,7},{5,6},{6,5},{7,4},{8,11},{9,10},{10,... | collective-permute-start | bytes 786440 | tf_op jit(solution)/shard_map/ppermute | solution.py:178
  10.7 19.5 %collective-permute-start.3 = (bf16[128,1024]{1,0:T(8,128)(2,1)S(1)}, bf16[128,1024]{1,0:T(8,128)(2,1)S(1)}, u32[]{:S(2)}, u32[]{:S(2)}) collective-permute-start(bf16[128,1024]{1,0:T(8,128)(2,1)S(1)} %get-tuple-element.28), channel_id=1, source_target_pairs={{0,1},{1,0},{2,3},{3,2},{4,5},{5,4},{6,7},{7,6},{8,9},{9,8},{10,11... | collective-permute-start | bytes 786440 | tf_op jit(solution)/shard_map/ppermute | solution.py:178
  10.7 21.0 %collective-permute-start.4 = (bf16[128,1024]{1,0:T(8,128)(2,1)S(1)}, bf16[128,1024]{1,0:T(8,128)(2,1)S(1)}, u32[]{:S(2)}, u32[]{:S(2)}) collective-permute-start(bf16[128,1024]{1,0:T(8,128)(2,1)S(1)} %get-tuple-element.30), channel_id=1, source_target_pairs={{0,2},{1,3},{2,0},{3,1},{4,6},{5,7},{6,4},{7,5},{8,10},{9,11},{10,... | collective-permute-start | bytes 786440 | tf_op jit(solution)/shard_map/ppermute | solution.py:178
  22.2 1.0 copy-start.6
  25.5 9.2 %collective-permute-start.2 = (bf16[256,128]{1,0:T(8,128)(2,1)}, bf16[256,128]{1,0:T(8,128)(2,1)S(1)}, u32[]{:S(2)}, u32[]{:S(2)}) collective-permute-start(bf16[256,128]{1,0:T(8,128)(2,1)} %attention.1.a0), channel_id=1, source_target_pairs={{0,3},{1,2},{2,1},{3,0},{4,7},{5,6},{6,5},{7,4},{8,11},{9,10},{10,... | collective-permute-start | bytes 196616 | tf_op jit(solution)/shard_map/ppermute | solution.py:191
  29.7 5.0 %collective-permute-start.1 = (bf16[256,128]{1,0:T(8,128)(2,1)}, bf16[256,128]{1,0:T(8,128)(2,1)S(1)}, u32[]{:S(2)}, u32[]{:S(2)}) collective-permute-start(bf16[256,128]{1,0:T(8,128)(2,1)} %attention.1.a0), channel_id=1, source_target_pairs={{0,2},{1,3},{2,0},{3,1},{4,6},{5,7},{6,4},{7,5},{8,10},{9,11},{10,... | collective-permute-start | bytes 196616 | tf_op jit(solution)/shard_map/ppermute | solution.py:191
  30.2 5.2 %copy-start.8 = (bf16[128,1024]{1,0:T(8,128)(2,1)}, bf16[128,1024]{1,0:T(8,128)(2,1)S(1)}, u32[]{:S(2)}) copy-start(bf16[128,1024]{1,0:T(8,128)(2,1)S(1)} %collective-permute-done.5.w3) | copy-start | bytes 786436
  30.2 4.5 %collective-permute-start = (bf16[256,128]{1,0:T(8,128)(2,1)}, bf16[256,128]{1,0:T(8,128)(2,1)S(1)}, u32[]{:S(2)}, u32[]{:S(2)}) collective-permute-start(bf16[256,128]{1,0:T(8,128)(2,1)} %attention.1.a0), channel_id=1, source_target_pairs={{0,1},{1,0},{2,3},{3,2},{4,5},{5,4},{6,7},{7,6},{8,9},{9,8},{10,11... | collective-permute-start | bytes 196616 | tf_op jit(solution)/shard_map/ppermute | solution.py:191
  30.2 5.2 %copy-start.9 = (bf16[128,1024]{1,0:T(8,128)(2,1)}, bf16[128,1024]{1,0:T(8,128)(2,1)S(1)}, u32[]{:S(2)}) copy-start(bf16[128,1024]{1,0:T(8,128)(2,1)S(1)} %collective-permute-done.3.w1) | copy-start | bytes 786436
  31.7 3.0 %copy-start.10 = (bf16[128,1024]{1,0:T(8,128)(2,1)}, bf16[128,1024]{1,0:T(8,128)(2,1)S(1)}, u32[]{:S(2)}) copy-start(bf16[128,1024]{1,0:T(8,128)(2,1)S(1)} %collective-permute-done.4.w2) | copy-start | bytes 786436
  35.4 94.1 %copy-start = (bf16[1,1,352,4096]{3,2,1,0:T(8,128)(2,1)S(1)}, bf16[1,1,352,4096]{3,2,1,0:T(8,128)(2,1)}, u32[]{:S(2)}) copy-start(bf16[1,1,352,4096]{3,2,1,0:T(8,128)(2,1)} %param.19) | copy-start | bytes 8650756
  100.0 25.3 %collective-permute-start.14 = (bf16[64,16,256]{2,1,0:T(8,128)(2,1)}, bf16[64,16,256]{2,1,0:T(8,128)(2,1)}, u32[]{:S(2)}, u32[]{:S(2)}) collective-permute-start(bf16[64,16,256]{2,1,0:T(8,128)(2,1)} %all_to_all.37.x0), channel_id=1, source_target_pairs={{0,96},{32,0},{64,32},{96,64},{1,97},{33,1},{65,33},{97,65},{2,98}... | collective-permute-start | bytes 1572872 | tf_op jit(solution)/shard_map/ppermute | solution.py:235
  102.5 22.9 %collective-permute-start.13 = (bf16[64,16,256]{2,1,0:T(8,128)(2,1)}, bf16[64,16,256]{2,1,0:T(8,128)(2,1)}, u32[]{:S(2)}, u32[]{:S(2)}) collective-permute-start(bf16[64,16,256]{2,1,0:T(8,128)(2,1)} %all_to_all.37.x0), channel_id=1, source_target_pairs={{0,64},{32,96},{64,0},{96,32},{1,65},{33,97},{65,1},{97,33},{2,66}... | collective-permute-start | bytes 1572872 | tf_op jit(solution)/shard_map/ppermute | solution.py:235
  102.9 26.6 %collective-permute-start.12 = (bf16[64,16,256]{2,1,0:T(8,128)(2,1)}, bf16[64,16,256]{2,1,0:T(8,128)(2,1)}, u32[]{:S(2)}, u32[]{:S(2)}) collective-permute-start(bf16[64,16,256]{2,1,0:T(8,128)(2,1)} %all_to_all.37.x0), channel_id=1, source_target_pairs={{0,32},{32,64},{64,96},{96,0},{1,33},{33,65},{65,97},{97,1},{2,34}... | collective-permute-start | bytes 1572872 | tf_op jit(solution)/shard_map/ppermute | solution.py:235
  103.7 38.8 %all-to-all-start.3 = ((bf16[64,16,256]{2,1,0:T(8,128)(2,1)}), bf16[64,16,256]{2,1,0:T(8,128)(2,1)S(1)}, u32[]{:S(2)}, u32[]{:S(2)}) async-start(bf16[64,16,256]{2,1,0:T(8,128)(2,1)} %get-tuple-element.17), calls=%async_computation.3 | async-start | bytes 1048576 | tf_op jit(solution)/shard_map/all_to_all | solution.py:234
  129.5 1.8 copy-start.1
  131.3 1.8 copy-start.3
  140.2 0.8 copy-start.5
  141.0 13.3 %collective-permute-start.15 = (bf16[64,16,256]{2,1,0:T(8,128)(2,1)}, bf16[64,16,256]{2,1,0:T(8,128)(2,1)}, u32[]{:S(2)}, u32[]{:S(2)}) collective-permute-start(bf16[64,16,256]{2,1,0:T(8,128)(2,1)} %get-tuple-element.24), channel_id=1, source_target_pairs={{0,96},{32,0},{64,32},{96,64},{1,97},{33,1},{65,33},{97,65},{2,98}... | collective-permute-start | bytes 1572872 | tf_op jit(solution)/shard_map/ppermute | solution.py:237
  141.0 14.2 %collective-permute-start.16 = (bf16[64,16,256]{2,1,0:T(8,128)(2,1)}, bf16[64,16,256]{2,1,0:T(8,128)(2,1)}, u32[]{:S(2)}, u32[]{:S(2)}) collective-permute-start(bf16[64,16,256]{2,1,0:T(8,128)(2,1)} %get-tuple-element.25), channel_id=1, source_target_pairs={{0,64},{32,96},{64,0},{96,32},{1,65},{33,97},{65,1},{97,33},{2,66}... | collective-permute-start | bytes 1572872 | tf_op jit(solution)/shard_map/ppermute | solution.py:237
  141.4 28.0 %collective-permute-start.17 = (bf16[64,16,256]{2,1,0:T(8,128)(2,1)}, bf16[64,16,256]{2,1,0:T(8,128)(2,1)}, u32[]{:S(2)}, u32[]{:S(2)}) collective-permute-start(bf16[64,16,256]{2,1,0:T(8,128)(2,1)} %get-tuple-element.26), channel_id=1, source_target_pairs={{0,32},{32,64},{64,96},{96,0},{1,33},{33,65},{65,97},{97,1},{2,34}... | collective-permute-start | bytes 1572872 | tf_op jit(solution)/shard_map/ppermute | solution.py:237
  142.5 34.9 %collective-permute-start.8 = (bf16[64,16,256]{2,1,0:T(8,128)(2,1)S(1)}, bf16[64,16,256]{2,1,0:T(8,128)(2,1)}, u32[]{:S(2)}, u32[]{:S(2)}) collective-permute-start(bf16[64,16,256]{2,1,0:T(8,128)(2,1)S(1)} %all-to-all-done.3.x0), channel_id=1, source_target_pairs={{0,96},{32,0},{64,32},{96,64},{1,97},{33,1},{65,33},{97,65},{2,98}... | collective-permute-start | bytes 1572872 | tf_op jit(solution)/shard_map/ppermute | solution.py:235
  144.9 32.9 %collective-permute-start.7 = (bf16[64,16,256]{2,1,0:T(8,128)(2,1)S(1)}, bf16[64,16,256]{2,1,0:T(8,128)(2,1)}, u32[]{:S(2)}, u32[]{:S(2)}) collective-permute-start(bf16[64,16,256]{2,1,0:T(8,128)(2,1)S(1)} %all-to-all-done.3.x0), channel_id=1, source_target_pairs={{0,64},{32,96},{64,0},{96,32},{1,65},{33,97},{65,1},{97,33},{2,66}... | collective-permute-start | bytes 1572872 | tf_op jit(solution)/shard_map/ppermute | solution.py:235
  154.3 35.9 %collective-permute-start.6 = (bf16[64,16,256]{2,1,0:T(8,128)(2,1)S(1)}, bf16[64,16,256]{2,1,0:T(8,128)(2,1)}, u32[]{:S(2)}, u32[]{:S(2)}) collective-permute-start(bf16[64,16,256]{2,1,0:T(8,128)(2,1)S(1)} %all-to-all-done.3.x0), channel_id=1, source_target_pairs={{0,32},{32,64},{64,96},{96,0},{1,33},{33,65},{65,97},{97,1},{2,34}... | collective-permute-start | bytes 1572872 | tf_op jit(solution)/shard_map/ppermute | solution.py:235
  172.0 55.1 %all-to-all-start.6 = ((bf16[64,16,256]{2,1,0:T(8,128)(2,1)}), bf16[64,16,256]{2,1,0:T(8,128)(2,1)}, u32[]{:S(2)}, u32[]{:S(2)}) async-start(bf16[64,16,256]{2,1,0:T(8,128)(2,1)} %add_convert_fusion), calls=%async_computation.6 | async-start | bytes 1048576 | tf_op jit(solution)/shard_map/all_to_all | solution.py:241
  190.3 1.8 copy-start.2
  192.1 1.8 copy-start.4
  199.9 12.9 %collective-permute-start.9 = (bf16[64,16,256]{2,1,0:T(8,128)(2,1)S(1)}, bf16[64,16,256]{2,1,0:T(8,128)(2,1)S(1)}, u32[]{:S(2)}, u32[]{:S(2)}) collective-permute-start(bf16[64,16,256]{2,1,0:T(8,128)(2,1)S(1)} %get-tuple-element.19), channel_id=1, source_target_pairs={{0,96},{32,0},{64,32},{96,64},{1,97},{33,1},{65,33},{97,65},{2,98}... | collective-permute-start | bytes 1572872 | tf_op jit(solution)/shard_map/ppermute | solution.py:237
  200.2 13.4 %collective-permute-start.10 = (bf16[64,16,256]{2,1,0:T(8,128)(2,1)S(1)}, bf16[64,16,256]{2,1,0:T(8,128)(2,1)S(1)}, u32[]{:S(2)}, u32[]{:S(2)}) collective-permute-start(bf16[64,16,256]{2,1,0:T(8,128)(2,1)S(1)} %get-tuple-element.20), channel_id=1, source_target_pairs={{0,64},{32,96},{64,0},{96,32},{1,65},{33,97},{65,1},{97,33},{2,66}... | collective-permute-start | bytes 1572872 | tf_op jit(solution)/shard_map/ppermute | solution.py:237
  200.6 26.2 %collective-permute-start.11 = (bf16[64,16,256]{2,1,0:T(8,128)(2,1)S(1)}, bf16[64,16,256]{2,1,0:T(8,128)(2,1)S(1)}, u32[]{:S(2)}, u32[]{:S(2)}) collective-permute-start(bf16[64,16,256]{2,1,0:T(8,128)(2,1)S(1)} %get-tuple-element.21), channel_id=1, source_target_pairs={{0,32},{32,64},{64,96},{96,0},{1,33},{33,65},{65,97},{97,1},{2,34}... | collective-permute-start | bytes 1572872 | tf_op jit(solution)/shard_map/ppermute | solution.py:237
  (3 other events, 2.0 us)

commit v2 on v1

v2 whole, which is shorter than its diff:
```python
import functools

import jax
import jax.numpy as jnp
from jax import lax
from jax.experimental import pallas as pl
from jax.experimental.pallas import tpu as pltpu
from jax.sharding import Mesh, PartitionSpec as P

CTX = ("xh", "y")
QUAD = ("xl", "core")
EXP = ("z", "xl", "core")
HOME = ("xh", "z", "xl", "core")

SUB = 16
LANE = 256

f32 = jnp.float32
bf16 = jnp.bfloat16
VMEM = pl.BlockSpec(memory_space=pltpu.VMEM)
SMEM = pl.BlockSpec(memory_space=pltpu.SMEM)
ANY = pl.BlockSpec(memory_space=pl.ANY)


def swap_matrix(outer, inner):
    size = outer * inner
    row = lax.broadcasted_iota(jnp.int32, (size, size), 0)
    col = lax.broadcasted_iota(jnp.int32, (size, size), 1)
    return (col == (row % inner) * outer + row // inner).astype(bf16)


def pack_kernel(keys, values, out_at, both, sent):
    head = keys.shape[1]
    both[:, :head] = keys[...]
    both[:, head:] = values[...]
    copies = [
        pltpu.make_async_copy(both, out_at.at[j], sent.at[j]) for j in range(out_at.shape[0])
    ]
    for copy in copies:
        copy.start()
    for copy in copies:
        copy.wait()


def attention_kernel(index, q_ref, kv_at, out_ref, kv_ref, arrived):
    own = index[0]

    def load(j):
        return pltpu.make_async_copy(kv_at.at[j], kv_ref.at[j], arrived.at[j])

    load(own).start()
    for j in range(kv_ref.shape[0]):

        @pl.when(j < own)
        def _():
            load(j).start()

    load(own).wait()
    q = q_ref[...]
    head = q.shape[1]
    scale = head ** (-0.5)

    def scores_of(j):
        return (
            lax.dot_general(
                q, kv_ref[j, :, :head], (((1,), (1,)), ((), ())), preferred_element_type=f32
            )
            * scale
        )

    scores = scores_of(own)
    row = lax.broadcasted_iota(jnp.int32, scores.shape, 0)
    col = lax.broadcasted_iota(jnp.int32, scores.shape, 1)
    scores = jnp.where(col <= row, scores, -1e30)
    top = jnp.max(scores, axis=1, keepdims=True)
    weights = jnp.exp(scores - top)
    total = jnp.sum(weights, axis=1, keepdims=True)
    acc = jnp.dot(weights.astype(bf16), kv_ref[own, :, head:], preferred_element_type=f32)

    def step(pair, carry):
        top, total, acc = carry
        blocks = (2 * pair, 2 * pair + 1)
        for j in blocks:

            @pl.when(j < own)
            def _():
                load(j).wait()

        scores = [jnp.where(j < own, scores_of(j), -1e30) for j in blocks]
        higher = jnp.maximum(top, jnp.max(jnp.maximum(*scores), axis=1, keepdims=True))
        fade = jnp.exp(top - higher)
        weights = [jnp.exp(part - higher) for part in scores]
        total = total * fade + jnp.sum(weights[0] + weights[1], axis=1, keepdims=True)
        acc = acc * fade
        for j, part in zip(blocks, weights):
            acc += jnp.dot(part.astype(bf16), kv_ref[j, :, head:], preferred_element_type=f32)
        return higher, total, acc

    top, total, acc = lax.fori_loop(0, (own + 1) // 2, step, (top, total, acc))
    out_ref[...] = (acc / total).astype(bf16)


def project_kernel(a0, a1, a2, a3, w0, w1, w2, w3, out_ref):
    heads = jnp.concatenate([a[...] for a in (a0, a1, a2, a3)], axis=1)
    weights = jnp.concatenate([w[...] for w in (w0, w1, w2, w3)], axis=0)
    out_ref[...] = jnp.dot(heads, weights, preferred_element_type=f32).astype(bf16)


def dispatch_kernel(ids, terms, stream, gain, hidden, outgoing, count, rows):
    tokens, width = stream.shape
    part = terms.shape[2]
    parts = width // part
    squares = jnp.zeros((tokens, 1), f32)
    for p in range(parts):
        cols = slice(p * part, (p + 1) * part)
        h = terms[p].astype(f32)
        for source in range(p + parts, terms.shape[0], parts):
            h += terms[source].astype(f32)
        h += stream[:, cols].astype(f32)
        hidden[:, cols] = h
        squares += jnp.sum(h * h, axis=1, keepdims=True)
    norm = lax.rsqrt(squares / width + 1e-06)
    blocks = []
    for k in range(SUB):
        cols = slice(k * LANE, (k + 1) * LANE)
        blocks.append(hidden[:, cols] * norm * gain[:, cols])
    normed = jnp.concatenate(blocks, axis=0).astype(bf16)
    swapped = jnp.dot(swap_matrix(tokens, SUB), normed, preferred_element_type=f32)
    rows[...] = swapped.astype(bf16).reshape(rows.shape)
    outgoing[...] = jnp.zeros_like(outgoing)
    for e in range(outgoing.shape[0] // 2):
        count[e] = 0
    for t in range(tokens):
        for k in range(ids.shape[1]):
            e = ids[t, k]
            seen = count[e]
            count[e] = seen + 1
            outgoing[2 * e + seen] = rows[t]


def expert_kernel(sizes_in, sizes_out, *refs):
    n_in, n_out = len(sizes_in), len(sizes_out)
    inputs, refs = refs[:n_in], refs[n_in:]
    stored, refs = refs[:3], refs[3:]
    outputs, refs = refs[:n_out], refs[n_out:]
    rows, gate_ref, up_ref, down_ref, flat, mixed, results, in_sem, weight_sem, out_sem = refs
    loads, at = [], 0
    for i, (source, size) in enumerate(zip(inputs, sizes_in)):
        loads.append(pltpu.make_async_copy(source, rows.at[at : at + size], in_sem.at[i]))
        loads[i].start()
        at += size
    weights = []
    for i, (source, target) in enumerate(zip(stored, (gate_ref, up_ref, down_ref))):
        weights.append(pltpu.make_async_copy(source, target, weight_sem.at[i]))
        weights[i].start()
    swap = swap_matrix(SUB, SUB)
    at = 0
    for load, size in zip(loads, sizes_in):
        load.wait()
        for start in range(at, at + size, SUB):
            block = rows[start : start + SUB].reshape(SUB * SUB, LANE)
            turned = jnp.dot(swap, block, preferred_element_type=f32).astype(bf16)
            for k in range(SUB):
                flat[start : start + SUB, k * LANE : (k + 1) * LANE] = turned[k * SUB : (k + 1) * SUB]
        at += size
    x = flat[...]
    weights[0].wait()
    gate = lax.dot_general(x, gate_ref[...], (((1,), (1,)), ((), ())), preferred_element_type=f32)
    weights[1].wait()
    up = lax.dot_general(x, up_ref[...], (((1,), (1,)), ((), ())), preferred_element_type=f32)
    activated = (gate / (1.0 + jnp.exp(-gate)) * up).astype(bf16)
    weights[2].wait()
    for k in range(SUB):
        down = jnp.dot(
            activated, down_ref[:, k * LANE : (k + 1) * LANE], preferred_element_type=f32
        ).astype(bf16)
        for g in range(at // SUB):
            mixed[g, k * SUB : (k + 1) * SUB, :] = down[g * SUB : (g + 1) * SUB]
    stores, at = [], 0
    for i, (target, size) in enumerate(zip(outputs, sizes_out)):
        for start in range(at, at + size, SUB):
            turned = jnp.dot(swap, mixed[start // SUB], preferred_element_type=f32).astype(bf16)
            results[start : start + SUB] = turned.reshape(SUB, SUB, LANE)
        stores.append(pltpu.make_async_copy(results.at[at : at + size], target, out_sem.at[i]))
        stores[i].start()
        at += size
    for store in stores:
        store.wait()


def total_kernel(*refs):
    pieces, out_ref = refs[:-1], refs[-1]
    each = len(pieces) // 2
    for slot in range(2):
        total = pieces[slot * each][...].astype(f32)
        for piece in pieces[slot * each + 1 : (slot + 1) * each]:
            total += piece[...].astype(f32)
        out_ref[:, slot * SUB : (slot + 1) * SUB] = total.astype(bf16)


def combine_kernel(ids, gates, hidden, routed, out_ref, count, total):
    tokens = hidden.shape[0]
    for e in range(routed.shape[0]):
        count[e] = 0
    for t in range(tokens):
        acc = jnp.zeros((SUB, LANE), f32)
        for k in range(ids.shape[1]):
            e = ids[t, k]
            seen = count[e]
            count[e] = seen + 1
            acc += gates[t, k] * routed[e, pl.ds(pl.multiple_of(seen * SUB, SUB), SUB)].astype(f32)
        for k in range(SUB):
            total[t : t + 1, k * LANE : (k + 1) * LANE] = acc[k : k + 1]
    out_ref[...] = (hidden[...] + total[...]).astype(bf16)


def shift(steps, count):
    return [(i, (i + steps) % count) for i in range(count)]


def flip(bits):
    return [(i, i ^ bits) for i in range(4)]


def on_device(
    stream_in, queries, keys, values, w_out, norm_gain, expert_ids, gates, w_gate, w_up, w_down
):
    shard, head = queries.shape
    tokens, width = stream_in.shape
    n_ctx = 8
    experts = 64
    hidden_units = w_gate.shape[2]
    quarter = width // 4
    place = lax.axis_index("xh") * 4 + lax.axis_index("y")
    quad = lax.axis_index(QUAD)

    weights = []
    for d in range(4):
        cols = lax.dynamic_slice_in_dim(w_out, (quad ^ d) * quarter, quarter, 1)
        weights.append(cols if d == 0 else lax.ppermute(cols, QUAD, flip(d)))

    copies = pl.pallas_call(
        pack_kernel,
        out_shape=jax.ShapeDtypeStruct((n_ctx, shard, 2 * head), bf16),
        in_specs=[VMEM, VMEM],
        out_specs=ANY,
        scratch_shapes=[pltpu.VMEM((shard, 2 * head), bf16), pltpu.SemaphoreType.DMA((n_ctx,))],
        name="pack",
    )(keys, values)
    everyone = lax.all_to_all(copies, CTX, 0, 0, tiled=True)
    attended = pl.pallas_call(
        attention_kernel,
        out_shape=jax.ShapeDtypeStruct((shard, head), bf16),
        in_specs=[SMEM, VMEM, ANY],
        out_specs=VMEM,
        scratch_shapes=[
            pltpu.VMEM((n_ctx, shard, 2 * head), bf16),
            pltpu.SemaphoreType.DMA((n_ctx,)),
        ],
        compiler_params=pltpu.CompilerParams(vmem_limit_bytes=8 * 1024 * 1024),
        name="attention",
    )(place.reshape(1).astype(jnp.int32), queries, everyone)

    heads = [attended] + [lax.ppermute(attended, QUAD, flip(d)) for d in (1, 2, 3)]
    term = pl.pallas_call(
        project_kernel,
        out_shape=jax.ShapeDtypeStruct((shard, quarter), bf16),
        in_specs=[VMEM] * 8,
        out_specs=VMEM,
        name="project",
    )(*heads, *weights)
    terms = lax.all_to_all(term.reshape(-1, tokens, quarter), EXP, 0, 0, tiled=True)

    slots = 2 * experts
    hidden, outgoing = pl.pallas_call(
        dispatch_kernel,
        out_shape=(
            jax.ShapeDtypeStruct((tokens, width), f32),
            jax.ShapeDtypeStruct((slots, SUB, LANE), bf16),
        ),
        in_specs=[SMEM, VMEM, VMEM, VMEM],
        out_specs=(VMEM, VMEM),
        scratch_shapes=[
            pltpu.SMEM((experts,), jnp.int32),
            pltpu.VMEM((tokens, SUB, LANE), bf16),
        ],
        name="dispatch",
    )(expert_ids, terms, stream_in, norm_gain.reshape(1, width))

    def home(rows):
        return lax.all_to_all(rows, HOME, 0, 0, tiled=True)

    def block(rows):
        return jax.ShapeDtypeStruct((rows, SUB, LANE), bf16)

    per = experts
    def expert_call(sizes_out, *inputs):
        sizes_in = tuple(x.shape[0] for x in inputs)
        total = sum(sizes_in)
        weight = pltpu.VMEM((hidden_units, width), bf16)
        return pl.pallas_call(
            functools.partial(expert_kernel, sizes_in, sizes_out),
            out_shape=tuple(block(size) for size in sizes_out),
            in_specs=[ANY] * (len(inputs) + 3),
            out_specs=(ANY,) * len(sizes_out),
            scratch_shapes=[
                pltpu.VMEM((total, SUB, LANE), bf16),
                weight,
                weight,
                weight,
                pltpu.VMEM((total, width), bf16),
                pltpu.VMEM((total // SUB, SUB * SUB, LANE), bf16),
                pltpu.VMEM((total, SUB, LANE), bf16),
                pltpu.SemaphoreType.DMA((len(sizes_in),)),
                pltpu.SemaphoreType.DMA((3,)),
                pltpu.SemaphoreType.DMA((len(sizes_out),)),
            ],
            compiler_params=pltpu.CompilerParams(vmem_limit_bytes=62 * 1024 * 1024),
            cost_estimate=pl.CostEstimate(
                flops=6 * total * hidden_units * width,
                bytes_accessed=6 * hidden_units * width,
                transcendentals=0,
            ),
            name="experts",
        )(*inputs, w_gate[0, 0], w_up[0, 0], w_down[0, 0])

    def up(rows):
        return lax.ppermute(rows, "y", shift(1, 4))

    def down(rows):
        return lax.ppermute(rows, "y", shift(-1, 4))

    def across(rows):
        return lax.ppermute(rows, "y", shift(2, 4))

    arrived = home(outgoing.reshape(experts, 2 * SUB, LANE))
    rows_a, rows_b = arrived[:, :SUB], arrived[:, SUB:]
    near = (up(rows_a), up(rows_b), down(rows_a), down(rows_b))
    own = expert_call((per, per), rows_a, rows_b)
    (below_a, below_b, above_a, above_b), own = lax.optimization_barrier((near, own))
    far = (down(above_a), up(below_b))
    early = expert_call((per,) * 4, below_a, above_a, below_b, above_b)
    early, far = lax.optimization_barrier((early, far))
    near_a = (down(early[0]), up(early[1]))
    late = expert_call((per, per), *far)
    near_a, late = lax.optimization_barrier((near_a, late))
    pieces = (own[0], *near_a, across(late[0]))
    pieces += (own[1], down(early[2]), up(early[3]), across(late[1]))
    part = experts // 4
    totals = pl.pallas_call(
        total_kernel,
        grid=(4,),
        out_shape=jax.ShapeDtypeStruct((experts, 2 * SUB, LANE), bf16),
        in_specs=[pl.BlockSpec((part, SUB, LANE), lambda i: (i, 0, 0))] * len(pieces),
        out_specs=pl.BlockSpec((part, 2 * SUB, LANE), lambda i: (i, 0, 0)),
        name="totals",
    )(*pieces)
    returned = home(totals)

    return pl.pallas_call(
        combine_kernel,
        out_shape=jax.ShapeDtypeStruct((tokens, width), bf16),
        in_specs=[SMEM, SMEM, VMEM, VMEM],
        out_specs=VMEM,
        scratch_shapes=[pltpu.SMEM((experts,), jnp.int32), pltpu.VMEM((tokens, width), f32)],
        name="combine",
    )(expert_ids, gates, hidden, returned)


def solution(mesh):
    fine = Mesh(mesh.devices.reshape(2, 4, 8, 2, 2), ("xh", "y", "z", "xl", "core"))
    token = CTX + EXP
    placed = (
        P(token, None),
        P(CTX, EXP),
        P(CTX, EXP),
        P(CTX, EXP),
        P(EXP, None),
        P(),
        P(token, None),
        P(token, None),
        P(CTX, EXP, None, None),
        P(CTX, EXP, None, None),
        P(CTX, EXP, None, None),
    )
    return jax.shard_map(
        on_device, mesh=fine, in_specs=placed, out_specs=P(token, None), check_vma=False
    )
```

time: 254 us -> 241 us (0.949)
  waiting for transfers between devices: 96.8 us -> 71 us
  blocking collectives: 81.7 us -> 101 us
  Pallas kernels: 23.5 us -> 38.6 us
  local copies, waits for them, and re-layouts: 11.7 us -> 3.13 us
  starting transfers between devices: 34.5 us -> 26.8 us
  other arithmetic: 3.93 us -> 0 us
    ppermute x12, waiting for transfers between devices: 81.2 us -> 52.7 us  [the longest x5 21 us: up(): return lax.ppermute(rows, 'y', shift(1, 4))]
    all_to_all x4 -> x3, blocking collectives: 81.7 us -> 101 us  [the longest x2 73.9 us: home(): return lax.all_to_all(rows, HOME, 0, 0, tiled=True)]
    pallas_call x2 -> x5, Pallas kernels: 13.1 us -> 30.7 us  [the longest x3 24.5 us: expert_call(): pl.pallas_call(functools.partial(expert_kernel, sizes_in, sizes_out), out...]
    all_to_all x2 -> x0, starting transfers between devices: 11.5 us -> none  [the longest x1 6.11 us: on_device(): own = lax.all_to_all(rows, HOME, 0, 0, tiled=True)]
    unnamed x28 -> x38, local copies, waits for them, and re-layouts: 9.71 us -> 2.24 us
    ppermute x3, waiting for transfers between devices: 1.51 us -> 5.96 us  [on_device(): weights.append(cols if d == 0 else lax.ppermute(cols, QUAD, flip(d)))]
    ppermute x12, starting transfers between devices: 10.2 us -> 13.3 us  [the longest x5 7.08 us: down(): return lax.ppermute(rows, 'y', shift(-1, 4))]
    convert_element_type x2 -> x0, other arithmetic: 2.88 us -> none  [on_device(): returned.append(lax.all_to_all(total.astype(bf16), HOME, 0, 0, tiled=True))]
  transfers between devices with their start and end apart: 21 -> 19, of which waited for: 13 -> 14; matrix products, arithmetic and copies ran while one was open for 1% -> 0% of each run, Pallas kernels for 6% -> 10%
where the time goes in v2:
time: 241 us; the launch traced here: 240 us
  blocking collectives  101 us (42%)
  waiting for transfers between devices  71 us (29%)
  Pallas kernels  38.6 us (16%)
  starting transfers between devices  26.8 us (11%)
  local copies, waits for them, and re-layouts  3.13 us (1%)
    all_to_all x2, blocking collectives, home(): return lax.all_to_all(rows, HOME, 0, 0, tiled=True)  73.9 us
    all_to_all x1, blocking collectives, on_device(): lax.all_to_all(term.reshape(-1, tokens, quarter), EXP, 0, 0, tiled=True)  26.8 us
    pallas_call x3, Pallas kernels, expert_call(): pl.pallas_call(functools.partial(expert_kernel, sizes_in, sizes_out), out...  24.5 us
    ppermute x5, waiting for transfers between devices, up(): return lax.ppermute(rows, 'y', shift(1, 4))  21 us
    ppermute x2, waiting for transfers between devices, across(): return lax.ppermute(rows, 'y', shift(2, 4))  20 us
    ppermute x5, waiting for transfers between devices, down(): return lax.ppermute(rows, 'y', shift(-1, 4))  11.7 us
    all_to_all x1, waiting for transfers between devices, on_device(): everyone = lax.all_to_all(copies, CTX, 0, 0, tiled=True)  11 us
    ppermute x5, starting transfers between devices, down(): return lax.ppermute(rows, 'y', shift(-1, 4))  7.08 us
  transfers between devices with their start and end apart: 19, of which 14 were waited for; matrix products, arithmetic and copies ran while one was open for 0% of the time, Pallas kernels for 10%

profile of v2, /device:TPU:3, one launch (start us, length us, event | category | flops | bytes accessed | tf_op | source)
XLA Modules:
  0.0 240.3 jit_solution(12709584986629575001)
XLA Ops:
  0.0 2.0 pack.1
  2.1 5.8 %all-to-all-start = ((bf16[8,256,256]{2,1,0:T(8,128)(2,1)}), bf16[8,256,256]{2,1,0:T(8,128)(2,1)S(1)}, u32[]{:S(2)}, u32[]{:S(2)}) async-start(bf16[8,256,256]{2,1,0:T(8,128)(2,1)} %pack.1), calls=%async_computation | async-start | bytes 2097152 | tf_op jit(solution)/shard_map/all_to_all | solution.py:250
  11.2 11.0 %all-to-all-done.kv_at = bf16[8,256,256]{2,1,0:T(8,128)(2,1)S(1)} async-done(((bf16[8,256,256]{2,1,0:T(8,128)(2,1)}), bf16[8,256,256]{2,1,0:T(8,128)(2,1)S(1)}, u32[]{:S(2)}, u32[]{:S(2)}) %all-to-all-start) | async-done | bytes 1048608 | tf_op jit(solution)/shard_map/all_to_all | solution.py:250
  22.9 3.4 %collective-permute-start = (bf16[256,128]{1,0:T(8,128)(2,1)S(1)}, bf16[256,128]{1,0:T(8,128)(2,1)S(1)}, u32[]{:S(2)}, u32[]{:S(2)}) collective-permute-start(bf16[256,128]{1,0:T(8,128)(2,1)S(1)} %attention.1.a0), channel_id=1, source_target_pairs={{0,1},{1,0},{2,3},{3,2},{4,5},{5,4},{6,7},{7,6},{8,9},{9,8},{10,11... | collective-permute-start | bytes 196616 | tf_op jit(solution)/shard_map/ppermute | solution.py:264
  28.1 6.0 %collective-permute-done.5.w3 = bf16[128,1024]{1,0:T(8,128)(2,1)S(1)} collective-permute-done((bf16[128,1024]{1,0:T(8,128)(2,1)S(1)}, bf16[128,1024]{1,0:T(8,128)(2,1)S(1)}, u32[]{:S(2)}, u32[]{:S(2)}) %collective-permute-start.5) | collective-permute-done | bytes 262176 | tf_op jit(solution)/shard_map/ppermute | solution.py:240
  34.1 1.3 collective-permute-done.2.a3
  36.0 2.6 %project.1 = bf16[256,1024]{1,0:T(8,128)(2,1)} custom-call(bf16[256,128]{1,0:T(8,128)(2,1)} %copy-done, bf16[256,128]{1,0:T(8,128)(2,1)} %copy-done.16, bf16[256,128]{1,0:T(8,128)(2,1)} %copy-done.17, bf16[256,128]{1,0:T(8,128)(2,1)} %copy-done.18, bf16[128,1024]{1,0:T(8,128)(2,1)} %get-tuple-element.61.w0, bf16[128,1024]{1,0:T(8,128)(2,1)} %copy-done.13, ...), custom_call_target="tpu_custom_call" | custom-call | tf_op jit(solution)/shard_map/project/pallas_call | solution.py:265
  38.6 26.8 %all_to_all.20.terms = bf16[32,8,1024]{2,1,0:T(8,128)(2,1)} all-to-all(bf16[32,8,1024]{2,1,0:T(8,128)(2,1)} %bitcast.16), channel_id=1, replica_groups=mesh['xh'=2,'y'=4,'z'=8,'xl'=2,'core'=2] {'z','xl','core'}, dimensions={0} | all-to-all | bytes 1048576 | tf_op jit(solution)/shard_map/all_to_all | solution.py:272
  65.4 2.4 %dispatch.1 = (f32[8,4096]{1,0:T(8,128)}, bf16[128,16,256]{2,1,0:T(8,128)(2,1)}) custom-call(s32[8,6]{1,0:T(8,128)} %ids.3, bf16[32,8,1024]{2,1,0:T(8,128)(2,1)} %all_to_all.20.terms, bf16[8,4096]{1,0:T(8,128)(2,1)} %stream.1, f32[1,4096]{1,0:T(1,128)} %bitcast.18), custom_call_target="tpu_custom_call" | custom-call | tf_op jit(solution)/shard_map/dispatch/pallas_call | solution.py:275
  67.8 36.4 %all_to_all.21 = bf16[64,32,256]{2,1,0:T(8,128)(2,1)S(1)} all-to-all(bf16[64,32,256]{2,1,0:T(8,128)(2,1)} %bitcast.17), channel_id=1, replica_groups=mesh['xh'=2,'y'=4,'z'=8,'xl'=2,'core'=2] {'xh','z','xl','core'}, dimensions={0} | all-to-all | bytes 2097152 | tf_op jit(solution)/shard_map/all_to_all | solution.py:291
  104.4 1.3 collective-permute-start.6
  105.6 1.2 collective-permute-start.7
  106.8 1.5 collective-permute-start.8
  108.6 7.8 %experts.3 = (bf16[64,16,256]{2,1,0:T(8,128)(2,1)}, bf16[64,16,256]{2,1,0:T(8,128)(2,1)}) custom-call(bf16[64,16,256]{2,1,0:T(8,128)(2,1)} %copy-done.3, bf16[64,16,256]{2,1,0:T(8,128)(2,1)} %copy-done.2, bf16[352,4096]{1,0:T(8,128)(2,1)} %bitcast.7, bf16[352,4096]{1,0:T(8,128)(2,1)} %bitcast.10, bf16[352,4096]{1,0:T(8,128)(2,1)} %bitcast.13), custom_call_target="tpu_custom_call" | custom-call | flops 1107296256 | bytes 8650752 | tf_op jit(solution)/shard_map/experts/pallas_call | solution.py:301
  116.4 3.2 %collective-permute-done.6.refs_0_ = bf16[64,16,256]{2,1,0:T(8,128)(2,1)} collective-permute-done((bf16[64,16,256]{2,1,0:T(8,128)(2,1)S(1)}, bf16[64,16,256]{2,1,0:T(8,128)(2,1)}, u32[]{:S(2)}, u32[]{:S(2)}) %collective-permute-start.6) | collective-permute-done | bytes 524320 | tf_op jit(solution)/shard_map/ppermute | solution.py:328
  119.6 9.9 %collective-permute-done.7.refs_2_ = bf16[64,16,256]{2,1,0:T(8,128)(2,1)S(1)} collective-permute-done((bf16[64,16,256]{2,1,0:T(8,128)(2,1)S(1)}, bf16[64,16,256]{2,1,0:T(8,128)(2,1)S(1)}, u32[]{:S(2)}, u32[]{:S(2)}) %collective-permute-start.7) | collective-permute-done | bytes 524320 | tf_op jit(solution)/shard_map/ppermute | solution.py:328
  129.5 1.8 collective-permute-done.9.refs_3_
  131.3 2.7 %collective-permute-start.10 = (bf16[64,16,256]{2,1,0:T(8,128)(2,1)}, bf16[64,16,256]{2,1,0:T(8,128)(2,1)S(1)}, u32[]{:S(2)}, u32[]{:S(2)}) collective-permute-start(bf16[64,16,256]{2,1,0:T(8,128)(2,1)} %collective-permute-done.8.refs_1_), channel_id=1, source_target_pairs={{0,96},{32,0},{64,32},{96,64},{1,97},{33,1},{65,33},{97,65},{2,98}... | collective-permute-start | bytes 1572872 | tf_op jit(solution)/shard_map/ppermute | solution.py:331
  134.0 8.9 %experts.4 = (bf16[64,16,256]{2,1,0:T(8,128)(2,1)}, bf16[64,16,256]{2,1,0:T(8,128)(2,1)}, bf16[64,16,256]{2,1,0:T(8,128)(2,1)}, bf16[64,16,256]{2,1,0:T(8,128)(2,1)}) custom-call(bf16[64,16,256]{2,1,0:T(8,128)(2,1)} %collective-permute-done.6.refs_0_, bf16[64,16,256]{2,1,0:T(8,128)(2,1)} %collective-permute-done.8.refs_1_, bf16[64,16,256]{2,1,0:T(8,128)(2,1)} %copy-done.12, ...), custom_call_target="tpu_custom_call" | custom-call | flops 2214592512 | bytes 8650752 | tf_op jit(solution)/shard_map/experts/pallas_call | solution.py:301
  143.0 2.4 %collective-permute-done.10.refs_0_ = bf16[64,16,256]{2,1,0:T(8,128)(2,1)S(1)} collective-permute-done((bf16[64,16,256]{2,1,0:T(8,128)(2,1)}, bf16[64,16,256]{2,1,0:T(8,128)(2,1)S(1)}, u32[]{:S(2)}, u32[]{:S(2)}) %collective-permute-start.10) | collective-permute-done | bytes 524320 | tf_op jit(solution)/shard_map/ppermute | solution.py:331
  145.4 2.8 %collective-permute-done.11.refs_1_ = bf16[64,16,256]{2,1,0:T(8,128)(2,1)S(1)} collective-permute-done((bf16[64,16,256]{2,1,0:T(8,128)(2,1)S(1)}, bf16[64,16,256]{2,1,0:T(8,128)(2,1)S(1)}, u32[]{:S(2)}, u32[]{:S(2)}) %collective-permute-start.11) | collective-permute-done | bytes 524320 | tf_op jit(solution)/shard_map/ppermute | solution.py:328
  150.4 1.9 collective-permute-start.15
  152.3 7.8 %experts.5 = (bf16[64,16,256]{2,1,0:T(8,128)(2,1)}, bf16[64,16,256]{2,1,0:T(8,128)(2,1)}) custom-call(bf16[64,16,256]{2,1,0:T(8,128)(2,1)} %copy-done.8, bf16[64,16,256]{2,1,0:T(8,128)(2,1)} %copy-done.9, bf16[352,4096]{1,0:T(8,128)(2,1)} %bitcast.9, bf16[352,4096]{1,0:T(8,128)(2,1)} %bitcast.12, bf16[352,4096]{1,0:T(8,128)(2,1)} %bitcast.15), custom_call_target="tpu_custom_call" | custom-call | flops 1107296256 | bytes 8650752 | tf_op jit(solution)/shard_map/experts/pallas_call | solution.py:301
  161.2 1.9 collective-permute-done.13.refs_2_
  163.1 3.0 %collective-permute-start.17 = (bf16[64,16,256]{2,1,0:T(8,128)(2,1)}, bf16[64,16,256]{2,1,0:T(8,128)(2,1)S(1)}, u32[]{:S(2)}, u32[]{:S(2)}) collective-permute-start(bf16[64,16,256]{2,1,0:T(8,128)(2,1)} %get-tuple-element.56), channel_id=1, source_target_pairs={{0,64},{32,96},{64,0},{96,32},{1,65},{33,97},{65,1},{97,33},{2,66}... | collective-permute-start | bytes 1572872 | tf_op jit(solution)/shard_map/ppermute | solution.py:334
  166.1 6.4 %collective-permute-done.15.refs_5_ = bf16[64,16,256]{2,1,0:T(8,128)(2,1)S(1)} collective-permute-done((bf16[64,16,256]{2,1,0:T(8,128)(2,1)}, bf16[64,16,256]{2,1,0:T(8,128)(2,1)S(1)}, u32[]{:S(2)}, u32[]{:S(2)}) %collective-permute-start.15) | collective-permute-done | bytes 524320 | tf_op jit(solution)/shard_map/ppermute | solution.py:331
  172.5 3.1 %collective-permute-done.16.refs_6_ = bf16[64,16,256]{2,1,0:T(8,128)(2,1)} collective-permute-done((bf16[64,16,256]{2,1,0:T(8,128)(2,1)}, bf16[64,16,256]{2,1,0:T(8,128)(2,1)}, u32[]{:S(2)}, u32[]{:S(2)}) %collective-permute-start.16) | collective-permute-done | bytes 524320 | tf_op jit(solution)/shard_map/ppermute | solution.py:328
  175.6 8.8 %collective-permute-done.14.refs_3_ = bf16[64,16,256]{2,1,0:T(8,128)(2,1)S(1)} collective-permute-done((bf16[64,16,256]{2,1,0:T(8,128)(2,1)}, bf16[64,16,256]{2,1,0:T(8,128)(2,1)S(1)}, u32[]{:S(2)}, u32[]{:S(2)}) %collective-permute-start.14) | collective-permute-done | bytes 524320 | tf_op jit(solution)/shard_map/ppermute | solution.py:334
  184.4 11.2 %collective-permute-done.17.refs_7_ = bf16[64,16,256]{2,1,0:T(8,128)(2,1)S(1)} collective-permute-done((bf16[64,16,256]{2,1,0:T(8,128)(2,1)}, bf16[64,16,256]{2,1,0:T(8,128)(2,1)S(1)}, u32[]{:S(2)}, u32[]{:S(2)}) %collective-permute-start.17) | collective-permute-done | bytes 524320 | tf_op jit(solution)/shard_map/ppermute | solution.py:334
  196.5 4.2 %totals.1 = bf16[64,32,256]{2,1,0:T(8,128)(2,1)} custom-call(bf16[64,16,256]{2,1,0:T(8,128)(2,1)} %get-tuple-element.35.refs_0_, bf16[64,16,256]{2,1,0:T(8,128)(2,1)} %copy-done.5, bf16[64,16,256]{2,1,0:T(8,128)(2,1)} %copy-done.6, bf16[64,16,256]{2,1,0:T(8,128)(2,1)} %copy-done.10, bf16[64,16,256]{2,1,0:T(8,128)(2,1)} %get-tuple-element.53.refs_4_, ...), custom_call_target="tpu_custom_call" | custom-call | tf_op jit(solution)/shard_map/totals/pallas_call | solution.py:350
  200.7 37.4 %all_to_all.22.routed = bf16[64,32,256]{2,1,0:T(8,128)(2,1)} all-to-all(bf16[64,32,256]{2,1,0:T(8,128)(2,1)} %totals.1), channel_id=1, replica_groups=mesh['xh'=2,'y'=4,'z'=8,'xl'=2,'core'=2] {'xh','z','xl','core'}, dimensions={0} | all-to-all | bytes 2097152 | tf_op jit(solution)/shard_map/all_to_all | solution.py:291
  238.1 2.2 combine.1
  (58 shorter events, 11.0 us)
Async XLA Ops:
  0.0 7.8 %copy-start.4 = (bf16[128,4096]{1,0:T(8,128)(2,1)S(1)}, bf16[128,4096]{1,0:T(8,128)(2,1)}, u32[]{:S(2)}) copy-start(bf16[128,4096]{1,0:T(8,128)(2,1)} %param.15) | copy-start | bytes 3145732
  0.0 22.2 %copy-start.1 = (bf16[256,128]{1,0:T(8,128)(2,1)S(1)}, bf16[256,128]{1,0:T(8,128)(2,1)}, u32[]{:S(2)}) copy-start(bf16[256,128]{1,0:T(8,128)(2,1)} %q_ref.1) | copy-start | bytes 196612
  2.1 20.1 %all-to-all-start = ((bf16[8,256,256]{2,1,0:T(8,128)(2,1)}), bf16[8,256,256]{2,1,0:T(8,128)(2,1)S(1)}, u32[]{:S(2)}, u32[]{:S(2)}) async-start(bf16[8,256,256]{2,1,0:T(8,128)(2,1)} %pack.1), calls=%async_computation | async-start | bytes 2097152 | tf_op jit(solution)/shard_map/all_to_all | solution.py:250
  8.6 18.7 %collective-permute-start.3 = (bf16[128,1024]{1,0:T(8,128)(2,1)S(1)}, bf16[128,1024]{1,0:T(8,128)(2,1)S(1)}, u32[]{:S(2)}, u32[]{:S(2)}) collective-permute-start(bf16[128,1024]{1,0:T(8,128)(2,1)S(1)} %get-tuple-element.60), channel_id=1, source_target_pairs={{0,1},{1,0},{2,3},{3,2},{4,5},{5,4},{6,7},{7,6},{8,9},{9,8},{10,11... | collective-permute-start | bytes 786440 | tf_op jit(solution)/shard_map/ppermute | solution.py:240
  9.6 18.5 %collective-permute-start.4 = (bf16[128,1024]{1,0:T(8,128)(2,1)S(1)}, bf16[128,1024]{1,0:T(8,128)(2,1)S(1)}, u32[]{:S(2)}, u32[]{:S(2)}) collective-permute-start(bf16[128,1024]{1,0:T(8,128)(2,1)S(1)} %get-tuple-element.62), channel_id=1, source_target_pairs={{0,2},{1,3},{2,0},{3,1},{4,6},{5,7},{6,4},{7,5},{8,10},{9,11},{10,... | collective-permute-start | bytes 786440 | tf_op jit(solution)/shard_map/ppermute | solution.py:240
  10.8 23.3 %collective-permute-start.5 = (bf16[128,1024]{1,0:T(8,128)(2,1)S(1)}, bf16[128,1024]{1,0:T(8,128)(2,1)S(1)}, u32[]{:S(2)}, u32[]{:S(2)}) collective-permute-start(bf16[128,1024]{1,0:T(8,128)(2,1)S(1)} %get-tuple-element.59), channel_id=1, source_target_pairs={{0,3},{1,2},{2,1},{3,0},{4,7},{5,6},{6,5},{7,4},{8,11},{9,10},{10,... | collective-permute-start | bytes 786440 | tf_op jit(solution)/shard_map/ppermute | solution.py:240
  22.9 12.5 %copy-start = (bf16[256,128]{1,0:T(8,128)(2,1)}, bf16[256,128]{1,0:T(8,128)(2,1)S(1)}, u32[]{:S(2)}) copy-start(bf16[256,128]{1,0:T(8,128)(2,1)S(1)} %attention.1.a0) | copy-start | bytes 196612
  22.9 11.1 %collective-permute-start = (bf16[256,128]{1,0:T(8,128)(2,1)S(1)}, bf16[256,128]{1,0:T(8,128)(2,1)S(1)}, u32[]{:S(2)}, u32[]{:S(2)}) collective-permute-start(bf16[256,128]{1,0:T(8,128)(2,1)S(1)} %attention.1.a0), channel_id=1, source_target_pairs={{0,1},{1,0},{2,3},{3,2},{4,5},{5,4},{6,7},{7,6},{8,9},{9,8},{10,11... | collective-permute-start | bytes 196616 | tf_op jit(solution)/shard_map/ppermute | solution.py:264
  26.3 7.7 %collective-permute-start.1 = (bf16[256,128]{1,0:T(8,128)(2,1)S(1)}, bf16[256,128]{1,0:T(8,128)(2,1)S(1)}, u32[]{:S(2)}, u32[]{:S(2)}) collective-permute-start(bf16[256,128]{1,0:T(8,128)(2,1)S(1)} %attention.1.a0), channel_id=1, source_target_pairs={{0,2},{1,3},{2,0},{3,1},{4,6},{5,7},{6,4},{7,5},{8,10},{9,11},{10,... | collective-permute-start | bytes 196616 | tf_op jit(solution)/shard_map/ppermute | solution.py:264
  27.3 8.1 %copy-start.13 = (bf16[128,1024]{1,0:T(8,128)(2,1)}, bf16[128,1024]{1,0:T(8,128)(2,1)S(1)}, u32[]{:S(2)}) copy-start(bf16[128,1024]{1,0:T(8,128)(2,1)S(1)} %collective-permute-done.3.w1) | copy-start | bytes 786436
  27.3 8.1 %collective-permute-start.2 = (bf16[256,128]{1,0:T(8,128)(2,1)S(1)}, bf16[256,128]{1,0:T(8,128)(2,1)S(1)}, u32[]{:S(2)}, u32[]{:S(2)}) collective-permute-start(bf16[256,128]{1,0:T(8,128)(2,1)S(1)} %attention.1.a0), channel_id=1, source_target_pairs={{0,3},{1,2},{2,1},{3,0},{4,7},{5,6},{6,5},{7,4},{8,11},{9,10},{10,... | collective-permute-start | bytes 196616 | tf_op jit(solution)/shard_map/ppermute | solution.py:264
  28.1 7.3 %copy-start.14 = (bf16[128,1024]{1,0:T(8,128)(2,1)}, bf16[128,1024]{1,0:T(8,128)(2,1)S(1)}, u32[]{:S(2)}) copy-start(bf16[128,1024]{1,0:T(8,128)(2,1)S(1)} %collective-permute-done.4.w2) | copy-start | bytes 786436
  104.3 4.2 %copy-start.2 = (bf16[64,16,256]{2,1,0:T(8,128)(2,1)}, bf16[64,16,256]{2,1,0:T(8,128)(2,1)S(1)}, u32[]{:S(2)}) copy-start(bf16[64,16,256]{2,1,0:T(8,128)(2,1)S(1)} %get-tuple-element.57.refs_1_) | copy-start | bytes 1572868
  104.3 4.2 %copy-start.3 = (bf16[64,16,256]{2,1,0:T(8,128)(2,1)}, bf16[64,16,256]{2,1,0:T(8,128)(2,1)S(1)}, u32[]{:S(2)}) copy-start(bf16[64,16,256]{2,1,0:T(8,128)(2,1)S(1)} %get-tuple-element.58.refs_0_) | copy-start | bytes 1572868
  104.4 15.2 %collective-permute-start.6 = (bf16[64,16,256]{2,1,0:T(8,128)(2,1)S(1)}, bf16[64,16,256]{2,1,0:T(8,128)(2,1)}, u32[]{:S(2)}, u32[]{:S(2)}) collective-permute-start(bf16[64,16,256]{2,1,0:T(8,128)(2,1)S(1)} %get-tuple-element.58.refs_0_), channel_id=1, source_target_pairs={{0,32},{32,64},{64,96},{96,0},{1,33},{33,65},{65,97},{97,1},{2,34}... | collective-permute-start | bytes 1572872 | tf_op jit(solution)/shard_map/ppermute | solution.py:328
  105.6 23.9 %collective-permute-start.7 = (bf16[64,16,256]{2,1,0:T(8,128)(2,1)S(1)}, bf16[64,16,256]{2,1,0:T(8,128)(2,1)S(1)}, u32[]{:S(2)}, u32[]{:S(2)}) collective-permute-start(bf16[64,16,256]{2,1,0:T(8,128)(2,1)S(1)} %get-tuple-element.57.refs_1_), channel_id=1, source_target_pairs={{0,32},{32,64},{64,96},{96,0},{1,33},{33,65},{65,97},{97,1},{2,34}... | collective-permute-start | bytes 1572872 | tf_op jit(solution)/shard_map/ppermute | solution.py:328
  106.8 22.7 %collective-permute-start.8 = (bf16[64,16,256]{2,1,0:T(8,128)(2,1)S(1)}, bf16[64,16,256]{2,1,0:T(8,128)(2,1)}, u32[]{:S(2)}, u32[]{:S(2)}) collective-permute-start(bf16[64,16,256]{2,1,0:T(8,128)(2,1)S(1)} %get-tuple-element.58.refs_0_), channel_id=1, source_target_pairs={{0,96},{32,0},{64,32},{96,64},{1,97},{33,1},{65,33},{97,65},{2,98}... | collective-permute-start | bytes 1572872 | tf_op jit(solution)/shard_map/ppermute | solution.py:331
  108.3 23.0 %collective-permute-start.9 = (bf16[64,16,256]{2,1,0:T(8,128)(2,1)S(1)}, bf16[64,16,256]{2,1,0:T(8,128)(2,1)}, u32[]{:S(2)}, u32[]{:S(2)}) collective-permute-start(bf16[64,16,256]{2,1,0:T(8,128)(2,1)S(1)} %get-tuple-element.57.refs_1_), channel_id=1, source_target_pairs={{0,96},{32,0},{64,32},{96,64},{1,97},{33,1},{65,33},{97,65},{2,98}... | collective-permute-start | bytes 1572872 | tf_op jit(solution)/shard_map/ppermute | solution.py:331
  129.5 4.5 %copy-start.12 = (bf16[64,16,256]{2,1,0:T(8,128)(2,1)}, bf16[64,16,256]{2,1,0:T(8,128)(2,1)S(1)}, u32[]{:S(2)}) copy-start(bf16[64,16,256]{2,1,0:T(8,128)(2,1)S(1)} %collective-permute-done.7.refs_2_) | copy-start | bytes 1572868
  131.3 14.1 %collective-permute-start.10 = (bf16[64,16,256]{2,1,0:T(8,128)(2,1)}, bf16[64,16,256]{2,1,0:T(8,128)(2,1)S(1)}, u32[]{:S(2)}, u32[]{:S(2)}) collective-permute-start(bf16[64,16,256]{2,1,0:T(8,128)(2,1)} %collective-permute-done.8.refs_1_), channel_id=1, source_target_pairs={{0,96},{32,0},{64,32},{96,64},{1,97},{33,1},{65,33},{97,65},{2,98}... | collective-permute-start | bytes 1572872 | tf_op jit(solution)/shard_map/ppermute | solution.py:331
  134.0 14.1 %collective-permute-start.11 = (bf16[64,16,256]{2,1,0:T(8,128)(2,1)S(1)}, bf16[64,16,256]{2,1,0:T(8,128)(2,1)S(1)}, u32[]{:S(2)}, u32[]{:S(2)}) collective-permute-start(bf16[64,16,256]{2,1,0:T(8,128)(2,1)S(1)} %collective-permute-done.7.refs_2_), channel_id=1, source_target_pairs={{0,32},{32,64},{64,96},{96,0},{1,33},{33,65},{65,97},{97,1},{2,34}... | collective-permute-start | bytes 1572872 | tf_op jit(solution)/shard_map/ppermute | solution.py:328
  145.4 2.8 %copy-start.8 = (bf16[64,16,256]{2,1,0:T(8,128)(2,1)}, bf16[64,16,256]{2,1,0:T(8,128)(2,1)S(1)}, u32[]{:S(2)}) copy-start(bf16[64,16,256]{2,1,0:T(8,128)(2,1)S(1)} %collective-permute-done.10.refs_0_) | copy-start | bytes 1572868
  148.9 12.2 %collective-permute-start.12 = (bf16[64,16,256]{2,1,0:T(8,128)(2,1)}, bf16[64,16,256]{2,1,0:T(8,128)(2,1)S(1)}, u32[]{:S(2)}, u32[]{:S(2)}) collective-permute-start(bf16[64,16,256]{2,1,0:T(8,128)(2,1)} %get-tuple-element.44), channel_id=1, source_target_pairs={{0,96},{32,0},{64,32},{96,64},{1,97},{33,1},{65,33},{97,65},{2,98}... | collective-permute-start | bytes 1572872 | tf_op jit(solution)/shard_map/ppermute | solution.py:331
  149.6 13.5 %collective-permute-start.13 = (bf16[64,16,256]{2,1,0:T(8,128)(2,1)}, bf16[64,16,256]{2,1,0:T(8,128)(2,1)S(1)}, u32[]{:S(2)}, u32[]{:S(2)}) collective-permute-start(bf16[64,16,256]{2,1,0:T(8,128)(2,1)} %get-tuple-element.45), channel_id=1, source_target_pairs={{0,32},{32,64},{64,96},{96,0},{1,33},{33,65},{65,97},{97,1},{2,34}... | collective-permute-start | bytes 1572872 | tf_op jit(solution)/shard_map/ppermute | solution.py:328
  150.4 22.1 %collective-permute-start.15 = (bf16[64,16,256]{2,1,0:T(8,128)(2,1)}, bf16[64,16,256]{2,1,0:T(8,128)(2,1)S(1)}, u32[]{:S(2)}, u32[]{:S(2)}) collective-permute-start(bf16[64,16,256]{2,1,0:T(8,128)(2,1)} %get-tuple-element.54), channel_id=1, source_target_pairs={{0,96},{32,0},{64,32},{96,64},{1,97},{33,1},{65,33},{97,65},{2,98}... | collective-permute-start | bytes 1572872 | tf_op jit(solution)/shard_map/ppermute | solution.py:331
  152.3 23.3 %collective-permute-start.16 = (bf16[64,16,256]{2,1,0:T(8,128)(2,1)}, bf16[64,16,256]{2,1,0:T(8,128)(2,1)}, u32[]{:S(2)}, u32[]{:S(2)}) collective-permute-start(bf16[64,16,256]{2,1,0:T(8,128)(2,1)} %get-tuple-element.55), channel_id=1, source_target_pairs={{0,32},{32,64},{64,96},{96,0},{1,33},{33,65},{65,97},{97,1},{2,34}... | collective-permute-start | bytes 1572872 | tf_op jit(solution)/shard_map/ppermute | solution.py:328
  161.2 34.5 %copy-start.5 = (bf16[64,16,256]{2,1,0:T(8,128)(2,1)}, bf16[64,16,256]{2,1,0:T(8,128)(2,1)S(1)}, u32[]{:S(2)}) copy-start(bf16[64,16,256]{2,1,0:T(8,128)(2,1)S(1)} %collective-permute-done.12.refs_1_) | copy-start | bytes 1572868
  163.1 32.5 %copy-start.6 = (bf16[64,16,256]{2,1,0:T(8,128)(2,1)}, bf16[64,16,256]{2,1,0:T(8,128)(2,1)S(1)}, u32[]{:S(2)}) copy-start(bf16[64,16,256]{2,1,0:T(8,128)(2,1)S(1)} %collective-permute-done.13.refs_2_) | copy-start | bytes 1572868
  163.1 21.3 %collective-permute-start.14 = (bf16[64,16,256]{2,1,0:T(8,128)(2,1)}, bf16[64,16,256]{2,1,0:T(8,128)(2,1)S(1)}, u32[]{:S(2)}, u32[]{:S(2)}) collective-permute-start(bf16[64,16,256]{2,1,0:T(8,128)(2,1)} %get-tuple-element.52), channel_id=1, source_target_pairs={{0,64},{32,96},{64,0},{96,32},{1,65},{33,97},{65,1},{97,33},{2,66}... | collective-permute-start | bytes 1572872 | tf_op jit(solution)/shard_map/ppermute | solution.py:334
  163.1 32.5 %collective-permute-start.17 = (bf16[64,16,256]{2,1,0:T(8,128)(2,1)}, bf16[64,16,256]{2,1,0:T(8,128)(2,1)S(1)}, u32[]{:S(2)}, u32[]{:S(2)}) collective-permute-start(bf16[64,16,256]{2,1,0:T(8,128)(2,1)} %get-tuple-element.56), channel_id=1, source_target_pairs={{0,64},{32,96},{64,0},{96,32},{1,65},{33,97},{65,1},{97,33},{2,66}... | collective-permute-start | bytes 1572872 | tf_op jit(solution)/shard_map/ppermute | solution.py:334
  172.5 23.2 %copy-start.7 = (bf16[64,16,256]{2,1,0:T(8,128)(2,1)}, bf16[64,16,256]{2,1,0:T(8,128)(2,1)S(1)}, u32[]{:S(2)}) copy-start(bf16[64,16,256]{2,1,0:T(8,128)(2,1)S(1)} %collective-permute-done.15.refs_5_) | copy-start | bytes 1572868
  184.4 11.2 %copy-start.10 = (bf16[64,16,256]{2,1,0:T(8,128)(2,1)}, bf16[64,16,256]{2,1,0:T(8,128)(2,1)S(1)}, u32[]{:S(2)}) copy-start(bf16[64,16,256]{2,1,0:T(8,128)(2,1)S(1)} %collective-permute-done.14.refs_3_) | copy-start | bytes 1572868
  (6 other events, 6.4 us)

commit v3 on v2

--- a/solution.py
+++ b/solution.py
@@ -188,14 +188,15 @@
         store.wait()
 
 
-def total_kernel(*refs):
-    pieces, out_ref = refs[:-1], refs[-1]
-    each = len(pieces) // 2
-    for slot in range(2):
-        total = pieces[slot * each][...].astype(f32)
-        for piece in pieces[slot * each + 1 : (slot + 1) * each]:
-            total += piece[...].astype(f32)
-        out_ref[:, slot * SUB : (slot + 1) * SUB] = total.astype(bf16)
+def relay_kernel(below, from_above, above, from_below, out_below, out_above):
+    out_below[...] = (below[...].astype(f32) + from_above[...].astype(f32)).astype(bf16)
+    out_above[...] = (above[...].astype(f32) + from_below[...].astype(f32)).astype(bf16)
+
+
+def total_kernel(a0, a1, a2, b0, b1, b2, out_ref):
+    for half, pieces in enumerate(((a0, a1, a2), (b0, b1, b2))):
+        total = pieces[0][...].astype(f32) + pieces[1][...].astype(f32)
+        out_ref[half] = (total + pieces[2][...].astype(f32)).astype(bf16)
 
 
 def combine_kernel(ids, gates, hidden, routed, out_ref, count, total):
@@ -267,6 +268,7 @@
         out_shape=jax.ShapeDtypeStruct((shard, quarter), bf16),
         in_specs=[VMEM] * 8,
         out_specs=VMEM,
+        compiler_params=pltpu.CompilerParams(vmem_limit_bytes=8 * 1024 * 1024),
         name="project",
     )(*heads, *weights)
     terms = lax.all_to_all(term.reshape(-1, tokens, quarter), EXP, 0, 0, tiled=True)
@@ -284,6 +286,7 @@
             pltpu.SMEM((experts,), jnp.int32),
             pltpu.VMEM((tokens, SUB, LANE), bf16),
         ],
+        compiler_params=pltpu.CompilerParams(vmem_limit_bytes=8 * 1024 * 1024),
         name="dispatch",
     )(expert_ids, terms, stream_in, norm_gain.reshape(1, width))
 
@@ -330,31 +333,41 @@
     def down(rows):
         return lax.ppermute(rows, "y", shift(-1, 4))
 
-    def across(rows):
-        return lax.ppermute(rows, "y", shift(2, 4))
-
-    arrived = home(outgoing.reshape(experts, 2 * SUB, LANE))
-    rows_a, rows_b = arrived[:, :SUB], arrived[:, SUB:]
-    near = (up(rows_a), up(rows_b), down(rows_a), down(rows_b))
-    own = expert_call((per, per), rows_a, rows_b)
-    (below_a, below_b, above_a, above_b), own = lax.optimization_barrier((near, own))
-    far = (down(above_a), up(below_b))
-    early = expert_call((per,) * 4, below_a, above_a, below_b, above_b)
+    arrived = home(outgoing.reshape(experts, 2 * SUB, LANE)).reshape(slots, SUB, LANE)
+    head, tail = arrived[:per], arrived[per:]
+    near = (up(head), down(tail), up(tail), down(head))
+    (own,) = expert_call((slots,), arrived)
+    (below_head, above_tail, below_tail, above_head), own = lax.optimization_barrier((near, own))
+    far = (up(below_head), down(above_tail))
+    early = expert_call((per,) * 4, below_head, below_tail, above_head, above_tail)
     early, far = lax.optimization_barrier((early, far))
-    near_a = (down(early[0]), up(early[1]))
+    ready = (down(early[0]), up(early[3]))
     late = expert_call((per, per), *far)
-    near_a, late = lax.optimization_barrier((near_a, late))
-    pieces = (own[0], *near_a, across(late[0]))
-    pieces += (own[1], down(early[2]), up(early[3]), across(late[1]))
-    part = experts // 4
+    ready, late = lax.optimization_barrier((ready, late))
+    sum_below, sum_above = pl.pallas_call(
+        relay_kernel,
+        out_shape=(block(per), block(per)),
+        in_specs=[VMEM] * 4,
+        out_specs=(VMEM, VMEM),
+        compiler_params=pltpu.CompilerParams(vmem_limit_bytes=8 * 1024 * 1024),
+        name="relay",
+    )(early[1], down(late[1]), early[2], up(late[0]))
+    rest = (down(sum_below), up(sum_above))
+    part = per // 2
+
+    def part_at(first):
+        return pl.BlockSpec((part, SUB, LANE), lambda i: (i + first, 0, 0))
+
     totals = pl.pallas_call(
         total_kernel,
-        grid=(4,),
-        out_shape=jax.ShapeDtypeStruct((experts, 2 * SUB, LANE), bf16),
-        in_specs=[pl.BlockSpec((part, SUB, LANE), lambda i: (i, 0, 0))] * len(pieces),
-        out_specs=pl.BlockSpec((part, 2 * SUB, LANE), lambda i: (i, 0, 0)),
+        grid=(2,),
+        out_shape=jax.ShapeDtypeStruct((2, per, SUB, LANE), bf16),
+        in_specs=[part_at(0)] * 3 + [part_at(2), part_at(0), part_at(0)],
+        out_specs=pl.BlockSpec((2, part, SUB, LANE), lambda i: (0, i, 0, 0)),
+        compiler_params=pltpu.CompilerParams(vmem_limit_bytes=12 * 1024 * 1024),
         name="totals",
-    )(*pieces)
+    )(own, ready[0], rest[1], own, rest[0], ready[1])
+    totals = totals.reshape(experts, 2 * SUB, LANE)
     returned = home(totals)
 
     return pl.pallas_call(
@@ -363,6 +376,7 @@
         in_specs=[SMEM, SMEM, VMEM, VMEM],
         out_specs=VMEM,
         scratch_shapes=[pltpu.SMEM((experts,), jnp.int32), pltpu.VMEM((tokens, width), f32)],
+        compiler_params=pltpu.CompilerParams(vmem_limit_bytes=8 * 1024 * 1024),
         name="combine",
     )(expert_ids, gates, hidden, returned)
 

time: 241 us -> 225 us (0.934)
  waiting for transfers between devices: 71 us -> 60.5 us
  Pallas kernels: 38.6 us -> 32.1 us
    ppermute x2 -> x0, waiting for transfers between devices: 20 us -> none  [across(): return lax.ppermute(rows, 'y', shift(2, 4))]
    ppermute x5 -> x6, waiting for transfers between devices: 21 us -> 28 us  [up(): return lax.ppermute(rows, 'y', shift(1, 4))]
    ppermute x5 -> x6, starting transfers between devices: 7.08 us -> 10.7 us  [down(): return lax.ppermute(rows, 'y', shift(-1, 4))]
    ppermute x2 -> x0, starting transfers between devices: 2.97 us -> none  [across(): return lax.ppermute(rows, 'y', shift(2, 4))]
    pallas_call x1 -> x2, Pallas kernels: 4.19 us -> 1.66 us  [the longest x1 1.42 us: on_device(): pl.pallas_call(total_kernel, grid=(2,), out_shape=jax.ShapeDtypeStruct((2...]
    ppermute x5 -> x6, waiting for transfers between devices: 11.7 us -> 13.7 us  [down(): return lax.ppermute(rows, 'y', shift(-1, 4))]
  transfers between devices with their start and end apart: 19 -> 19, of which waited for: 14 -> 13; matrix products, arithmetic and copies ran while one was open for 0% -> 0% of each run, Pallas kernels for 10% -> 11%
where the time goes in v3:
time: 225 us; the launch traced here: 224 us
  blocking collectives  99.5 us (44%)
  waiting for transfers between devices  60.5 us (27%)
  Pallas kernels  32.1 us (14%)
  starting transfers between devices  28.1 us (12%)
  local copies, waits for them, and re-layouts  4.15 us (2%)
    all_to_all x2, blocking collectives, home(): return lax.all_to_all(rows, HOME, 0, 0, tiled=True)  73 us
    ppermute x6, waiting for transfers between devices, up(): return lax.ppermute(rows, 'y', shift(1, 4))  28 us
    all_to_all x1, blocking collectives, on_device(): lax.all_to_all(term.reshape(-1, tokens, quarter), EXP, 0, 0, tiled=True)  26.5 us
    pallas_call x3, Pallas kernels, expert_call(): pl.pallas_call(functools.partial(expert_kernel, sizes_in, sizes_out), out...  24.8 us
    ppermute x6, waiting for transfers between devices, down(): return lax.ppermute(rows, 'y', shift(-1, 4))  13.7 us
    all_to_all x1, waiting for transfers between devices, on_device(): everyone = lax.all_to_all(copies, CTX, 0, 0, tiled=True)  11.5 us
    ppermute x6, starting transfers between devices, down(): return lax.ppermute(rows, 'y', shift(-1, 4))  10.7 us
    ppermute x3, waiting for transfers between devices, on_device(): weights.append(cols if d == 0 else lax.ppermute(cols, QUAD, flip(d)))  5.97 us
  transfers between devices with their start and end apart: 19, of which 13 were waited for; matrix products, arithmetic and copies ran while one was open for 0% of the time, Pallas kernels for 11%

profile of v3, /device:TPU:3, one launch (start us, length us, event | category | flops | bytes accessed | tf_op | source)
XLA Modules:
  0.0 224.5 jit_solution(18392532331656353683)
XLA Ops:
  0.0 2.0 pack.1
  2.0 5.8 %all-to-all-start = ((bf16[8,256,256]{2,1,0:T(8,128)(2,1)}), bf16[8,256,256]{2,1,0:T(8,128)(2,1)S(1)}, u32[]{:S(2)}, u32[]{:S(2)}) async-start(bf16[8,256,256]{2,1,0:T(8,128)(2,1)} %pack.1), calls=%async_computation | async-start | bytes 2097152 | tf_op jit(solution)/shard_map/all_to_all | solution.py:251
  7.9 1.0 collective-permute-start.3
  9.0 1.2 collective-permute-start.4
  10.7 11.5 %all-to-all-done.kv_at = bf16[8,256,256]{2,1,0:T(8,128)(2,1)S(1)} async-done(((bf16[8,256,256]{2,1,0:T(8,128)(2,1)}), bf16[8,256,256]{2,1,0:T(8,128)(2,1)S(1)}, u32[]{:S(2)}, u32[]{:S(2)}) %all-to-all-start) | async-done | bytes 1048608 | tf_op jit(solution)/shard_map/all_to_all | solution.py:251
  22.9 3.4 %collective-permute-start = (bf16[256,128]{1,0:T(8,128)(2,1)S(1)}, bf16[256,128]{1,0:T(8,128)(2,1)S(1)}, u32[]{:S(2)}, u32[]{:S(2)}) collective-permute-start(bf16[256,128]{1,0:T(8,128)(2,1)S(1)} %attention.1.a0), channel_id=1, source_target_pairs={{0,1},{1,0},{2,3},{3,2},{4,5},{5,4},{6,7},{7,6},{8,9},{9,8},{10,11... | collective-permute-start | bytes 196616 | tf_op jit(solution)/shard_map/ppermute | solution.py:265
  28.1 6.0 %collective-permute-done.5.w3 = bf16[128,1024]{1,0:T(8,128)(2,1)S(1)} collective-permute-done((bf16[128,1024]{1,0:T(8,128)(2,1)S(1)}, bf16[128,1024]{1,0:T(8,128)(2,1)S(1)}, u32[]{:S(2)}, u32[]{:S(2)}) %collective-permute-start.5) | collective-permute-done | bytes 262176 | tf_op jit(solution)/shard_map/ppermute | solution.py:241
  34.0 1.4 collective-permute-done.2.a3
  35.8 26.5 %all_to_all.20.terms = bf16[32,8,1024]{2,1,0:T(8,128)(2,1)S(1)} all-to-all(bf16[32,8,1024]{2,1,0:T(8,128)(2,1)S(1)} %bitcast.12), channel_id=1, replica_groups=mesh['xh'=2,'y'=4,'z'=8,'xl'=2,'core'=2] {'z','xl','core'}, dimensions={0} | all-to-all | bytes 1048576 | tf_op jit(solution)/shard_map/all_to_all | solution.py:274
  63.3 36.2 %all_to_all.21 = bf16[64,32,256]{2,1,0:T(8,128)(2,1)S(1)} all-to-all(bf16[64,32,256]{2,1,0:T(8,128)(2,1)S(1)} %bitcast.13), channel_id=1, replica_groups=mesh['xh'=2,'y'=4,'z'=8,'xl'=2,'core'=2] {'xh','z','xl','core'}, dimensions={0} | all-to-all | bytes 2097152 | tf_op jit(solution)/shard_map/all_to_all | solution.py:294
  100.5 1.2 collective-permute-start.6
  101.7 1.5 collective-permute-start.7
  103.2 2.7 %collective-permute-start.9 = (bf16[64,16,256]{2,1,0:T(8,128)(2,1)S(1)}, bf16[64,16,256]{2,1,0:T(8,128)(2,1)}, u32[]{:S(2)}, u32[]{:S(2)}) collective-permute-start(bf16[64,16,256]{2,1,0:T(8,128)(2,1)S(1)} %bitcast.26), channel_id=1, source_target_pairs={{0,96},{32,0},{64,32},{96,64},{1,97},{33,1},{65,33},{97,65},{2,98}... | collective-permute-start | bytes 1572872 | tf_op jit(solution)/shard_map/ppermute | solution.py:334
  105.8 8.1 %experts.3.a0.b0 = bf16[128,16,256]{2,1,0:T(8,128)(2,1)} custom-call(bf16[128,16,256]{2,1,0:T(8,128)(2,1)} %bitcast.24, bf16[352,4096]{1,0:T(8,128)(2,1)} %bitcast.15, bf16[352,4096]{1,0:T(8,128)(2,1)} %bitcast.18, bf16[352,4096]{1,0:T(8,128)(2,1)} %bitcast.21), custom_call_target="tpu_custom_call" | custom-call | flops 1107296256 | bytes 8650752 | tf_op jit(solution)/shard_map/experts/pallas_call | solution.py:304
  113.9 1.8 collective-permute-done.6.refs_0_
  115.9 9.7 %collective-permute-done.8.refs_1_ = bf16[64,16,256]{2,1,0:T(8,128)(2,1)} collective-permute-done((bf16[64,16,256]{2,1,0:T(8,128)(2,1)}, bf16[64,16,256]{2,1,0:T(8,128)(2,1)}, u32[]{:S(2)}, u32[]{:S(2)}) %collective-permute-start.8) | collective-permute-done | bytes 524320 | tf_op jit(solution)/shard_map/ppermute | solution.py:331
  126.1 1.2 collective-permute-start.10
  127.3 1.5 collective-permute-start.11
  128.8 8.9 %experts.4 = (bf16[64,16,256]{2,1,0:T(8,128)(2,1)}, bf16[64,16,256]{2,1,0:T(8,128)(2,1)}, bf16[64,16,256]{2,1,0:T(8,128)(2,1)}, bf16[64,16,256]{2,1,0:T(8,128)(2,1)}) custom-call(bf16[64,16,256]{2,1,0:T(8,128)(2,1)} %collective-permute-done.6.refs_0_, bf16[64,16,256]{2,1,0:T(8,128)(2,1)} %collective-permute-done.8.refs_1_, ...), custom_call_target="tpu_custom_call" | custom-call | flops 2214592512 | bytes 8650752 | tf_op jit(solution)/shard_map/experts/pallas_call | solution.py:304
  137.7 3.5 %collective-permute-done.10.refs_0_ = bf16[64,16,256]{2,1,0:T(8,128)(2,1)S(1)} collective-permute-done((bf16[64,16,256]{2,1,0:T(8,128)(2,1)}, bf16[64,16,256]{2,1,0:T(8,128)(2,1)S(1)}, u32[]{:S(2)}, u32[]{:S(2)}) %collective-permute-start.10) | collective-permute-done | bytes 524320 | tf_op jit(solution)/shard_map/ppermute | solution.py:331
  142.2 2.2 collective-permute-start.12
  144.3 7.8 %experts.5 = (bf16[64,16,256]{2,1,0:T(8,128)(2,1)}, bf16[64,16,256]{2,1,0:T(8,128)(2,1)}) custom-call(bf16[64,16,256]{2,1,0:T(8,128)(2,1)} %copy-done.10, bf16[64,16,256]{2,1,0:T(8,128)(2,1)} %copy-done.11, bf16[352,4096]{1,0:T(8,128)(2,1)} %bitcast.17, bf16[352,4096]{1,0:T(8,128)(2,1)} %bitcast.20, bf16[352,4096]{1,0:T(8,128)(2,1)} %bitcast.23), custom_call_target="tpu_custom_call" | custom-call | flops 1107296256 | bytes 8650752 | tf_op jit(solution)/shard_map/experts/pallas_call | solution.py:304
  152.2 3.1 %collective-permute-done.12.a1 = bf16[64,16,256]{2,1,0:T(8,128)(2,1)S(1)} collective-permute-done((bf16[64,16,256]{2,1,0:T(8,128)(2,1)}, bf16[64,16,256]{2,1,0:T(8,128)(2,1)S(1)}, u32[]{:S(2)}, u32[]{:S(2)}) %collective-permute-start.12) | collective-permute-done | bytes 524320 | tf_op jit(solution)/shard_map/ppermute | solution.py:334
  155.3 2.7 %collective-permute-done.13.b2 = bf16[64,16,256]{2,1,0:T(8,128)(2,1)} collective-permute-done((bf16[64,16,256]{2,1,0:T(8,128)(2,1)}, bf16[64,16,256]{2,1,0:T(8,128)(2,1)}, u32[]{:S(2)}, u32[]{:S(2)}) %collective-permute-start.13) | collective-permute-done | bytes 524320 | tf_op jit(solution)/shard_map/ppermute | solution.py:331
  158.2 1.3 collective-permute-start.15
  159.5 9.9 %collective-permute-done.14.from_above = bf16[64,16,256]{2,1,0:T(8,128)(2,1)S(1)} collective-permute-done((bf16[64,16,256]{2,1,0:T(8,128)(2,1)}, bf16[64,16,256]{2,1,0:T(8,128)(2,1)S(1)}, u32[]{:S(2)}, u32[]{:S(2)}) %collective-permute-start.14) | collective-permute-done | bytes 524320 | tf_op jit(solution)/shard_map/ppermute | solution.py:334
  169.4 1.4 collective-permute-done.15.from_below
  173.2 2.7 %collective-permute-start.17 = (bf16[64,16,256]{2,1,0:T(8,128)(2,1)S(1)}, bf16[64,16,256]{2,1,0:T(8,128)(2,1)S(1)}, u32[]{:S(2)}, u32[]{:S(2)}) collective-permute-start(bf16[64,16,256]{2,1,0:T(8,128)(2,1)S(1)} %get-tuple-element.53), channel_id=1, source_target_pairs={{0,96},{32,0},{64,32},{96,64},{1,97},{33,1},{65,33},{97,65},{2,98}... | collective-permute-start | bytes 1572872 | tf_op jit(solution)/shard_map/ppermute | solution.py:334
  175.9 8.8 %collective-permute-done.16.a2 = bf16[64,16,256]{2,1,0:T(8,128)(2,1)S(1)} collective-permute-done((bf16[64,16,256]{2,1,0:T(8,128)(2,1)S(1)}, bf16[64,16,256]{2,1,0:T(8,128)(2,1)S(1)}, u32[]{:S(2)}, u32[]{:S(2)}) %collective-permute-start.16) | collective-permute-done | bytes 524320 | tf_op jit(solution)/shard_map/ppermute | solution.py:331
  184.7 1.4 totals.1
  186.1 36.8 %all_to_all.22.routed = bf16[64,32,256]{2,1,0:T(8,128)(2,1)S(1)} all-to-all(bf16[64,32,256]{2,1,0:T(8,128)(2,1)S(1)} %bitcast.11), channel_id=1, replica_groups=mesh['xh'=2,'y'=4,'z'=8,'xl'=2,'core'=2] {'xh','z','xl','core'}, dimensions={0} | all-to-all | bytes 2097152 | tf_op jit(solution)/shard_map/all_to_all | solution.py:294
  222.9 1.6 combine.1
  (45 shorter events, 9.7 us)
Async XLA Ops:
  0.0 7.8 %copy-start.9 = (bf16[128,4096]{1,0:T(8,128)(2,1)S(1)}, bf16[128,4096]{1,0:T(8,128)(2,1)}, u32[]{:S(2)}) copy-start(bf16[128,4096]{1,0:T(8,128)(2,1)} %param.15) | copy-start | bytes 3145732
  0.0 22.2 %copy-start.3 = (bf16[256,128]{1,0:T(8,128)(2,1)S(1)}, bf16[256,128]{1,0:T(8,128)(2,1)}, u32[]{:S(2)}) copy-start(bf16[256,128]{1,0:T(8,128)(2,1)} %q_ref.1) | copy-start | bytes 196612
  2.0 20.1 %all-to-all-start = ((bf16[8,256,256]{2,1,0:T(8,128)(2,1)}), bf16[8,256,256]{2,1,0:T(8,128)(2,1)S(1)}, u32[]{:S(2)}, u32[]{:S(2)}) async-start(bf16[8,256,256]{2,1,0:T(8,128)(2,1)} %pack.1), calls=%async_computation | async-start | bytes 2097152 | tf_op jit(solution)/shard_map/all_to_all | solution.py:251
  7.8 54.5 %copy-start.4 = (bf16[8,4096]{1,0:T(8,128)(2,1)S(1)}, bf16[8,4096]{1,0:T(8,128)(2,1)}, u32[]{:S(2)}) copy-start(bf16[8,4096]{1,0:T(8,128)(2,1)} %stream.1) | copy-start | bytes 196612
  7.8 54.5 %copy-start.5 = (s32[8,6]{1,0:T(8,128)S(1)}, s32[8,6]{1,0:T(8,128)}, u32[]{:S(2)}) copy-start(s32[8,6]{1,0:T(8,128)} %ids.3) | copy-start | bytes 580
  7.8 54.5 %copy-start.6 = (f32[4096]{0:T(1024)S(1)}, f32[4096]{0:T(1024)}, u32[]{:S(2)}) copy-start(f32[4096]{0:T(1024)} %param.16) | copy-start | bytes 49156
  7.9 19.4 %collective-permute-start.3 = (bf16[128,1024]{1,0:T(8,128)(2,1)S(1)}, bf16[128,1024]{1,0:T(8,128)(2,1)S(1)}, u32[]{:S(2)}, u32[]{:S(2)}) collective-permute-start(bf16[128,1024]{1,0:T(8,128)(2,1)S(1)} %get-tuple-element.58), channel_id=1, source_target_pairs={{0,1},{1,0},{2,3},{3,2},{4,5},{5,4},{6,7},{7,6},{8,9},{9,8},{10,11... | collective-permute-start | bytes 786440 | tf_op jit(solution)/shard_map/ppermute | solution.py:241
  9.0 19.1 %collective-permute-start.4 = (bf16[128,1024]{1,0:T(8,128)(2,1)S(1)}, bf16[128,1024]{1,0:T(8,128)(2,1)S(1)}, u32[]{:S(2)}, u32[]{:S(2)}) collective-permute-start(bf16[128,1024]{1,0:T(8,128)(2,1)S(1)} %get-tuple-element.60), channel_id=1, source_target_pairs={{0,2},{1,3},{2,0},{3,1},{4,6},{5,7},{6,4},{7,5},{8,10},{9,11},{10,... | collective-permute-start | bytes 786440 | tf_op jit(solution)/shard_map/ppermute | solution.py:241
  10.2 23.9 %collective-permute-start.5 = (bf16[128,1024]{1,0:T(8,128)(2,1)S(1)}, bf16[128,1024]{1,0:T(8,128)(2,1)S(1)}, u32[]{:S(2)}, u32[]{:S(2)}) collective-permute-start(bf16[128,1024]{1,0:T(8,128)(2,1)S(1)} %get-tuple-element.57), channel_id=1, source_target_pairs={{0,3},{1,2},{2,1},{3,0},{4,7},{5,6},{6,5},{7,4},{8,11},{9,10},{10,... | collective-permute-start | bytes 786440 | tf_op jit(solution)/shard_map/ppermute | solution.py:241
  22.9 11.1 %collective-permute-start = (bf16[256,128]{1,0:T(8,128)(2,1)S(1)}, bf16[256,128]{1,0:T(8,128)(2,1)S(1)}, u32[]{:S(2)}, u32[]{:S(2)}) collective-permute-start(bf16[256,128]{1,0:T(8,128)(2,1)S(1)} %attention.1.a0), channel_id=1, source_target_pairs={{0,1},{1,0},{2,3},{3,2},{4,5},{5,4},{6,7},{7,6},{8,9},{9,8},{10,11... | collective-permute-start | bytes 196616 | tf_op jit(solution)/shard_map/ppermute | solution.py:265
  26.3 7.7 %collective-permute-start.1 = (bf16[256,128]{1,0:T(8,128)(2,1)S(1)}, bf16[256,128]{1,0:T(8,128)(2,1)S(1)}, u32[]{:S(2)}, u32[]{:S(2)}) collective-permute-start(bf16[256,128]{1,0:T(8,128)(2,1)S(1)} %attention.1.a0), channel_id=1, source_target_pairs={{0,2},{1,3},{2,0},{3,1},{4,6},{5,7},{6,4},{7,5},{8,10},{9,11},{10,... | collective-permute-start | bytes 196616 | tf_op jit(solution)/shard_map/ppermute | solution.py:265
  27.3 8.1 %collective-permute-start.2 = (bf16[256,128]{1,0:T(8,128)(2,1)S(1)}, bf16[256,128]{1,0:T(8,128)(2,1)S(1)}, u32[]{:S(2)}, u32[]{:S(2)}) collective-permute-start(bf16[256,128]{1,0:T(8,128)(2,1)S(1)} %attention.1.a0), channel_id=1, source_target_pairs={{0,3},{1,2},{2,1},{3,0},{4,7},{5,6},{6,5},{7,4},{8,11},{9,10},{10,... | collective-permute-start | bytes 196616 | tf_op jit(solution)/shard_map/ppermute | solution.py:265
  99.5 6.3 %copy-start.8 = (bf16[64,32,256]{2,1,0:T(8,128)(2,1)}, bf16[64,32,256]{2,1,0:T(8,128)(2,1)S(1)}, u32[]{:S(2)}) copy-start(bf16[64,32,256]{2,1,0:T(8,128)(2,1)S(1)} %all_to_all.21) | copy-start | bytes 3145732
  100.5 15.3 %collective-permute-start.6 = (bf16[64,16,256]{2,1,0:T(8,128)(2,1)S(1)}, bf16[64,16,256]{2,1,0:T(8,128)(2,1)}, u32[]{:S(2)}, u32[]{:S(2)}) collective-permute-start(bf16[64,16,256]{2,1,0:T(8,128)(2,1)S(1)} %bitcast.25), channel_id=1, source_target_pairs={{0,32},{32,64},{64,96},{96,0},{1,33},{33,65},{65,97},{97,1},{2,34}... | collective-permute-start | bytes 1572872 | tf_op jit(solution)/shard_map/ppermute | solution.py:331
  101.7 14.2 %collective-permute-start.7 = (bf16[64,16,256]{2,1,0:T(8,128)(2,1)}, bf16[64,16,256]{2,1,0:T(8,128)(2,1)}, u32[]{:S(2)}, u32[]{:S(2)}) collective-permute-start(bf16[64,16,256]{2,1,0:T(8,128)(2,1)} %bitcast.5), channel_id=1, source_target_pairs={{0,96},{32,0},{64,32},{96,64},{1,97},{33,1},{65,33},{97,65},{2,98}... | collective-permute-start | bytes 1572872 | tf_op jit(solution)/shard_map/ppermute | solution.py:334
  103.2 22.5 %collective-permute-start.8 = (bf16[64,16,256]{2,1,0:T(8,128)(2,1)}, bf16[64,16,256]{2,1,0:T(8,128)(2,1)}, u32[]{:S(2)}, u32[]{:S(2)}) collective-permute-start(bf16[64,16,256]{2,1,0:T(8,128)(2,1)} %bitcast.5), channel_id=1, source_target_pairs={{0,32},{32,64},{64,96},{96,0},{1,33},{33,65},{65,97},{97,1},{2,34}... | collective-permute-start | bytes 1572872 | tf_op jit(solution)/shard_map/ppermute | solution.py:331
  103.2 22.9 %collective-permute-start.9 = (bf16[64,16,256]{2,1,0:T(8,128)(2,1)S(1)}, bf16[64,16,256]{2,1,0:T(8,128)(2,1)}, u32[]{:S(2)}, u32[]{:S(2)}) collective-permute-start(bf16[64,16,256]{2,1,0:T(8,128)(2,1)S(1)} %bitcast.26), channel_id=1, source_target_pairs={{0,96},{32,0},{64,32},{96,64},{1,97},{33,1},{65,33},{97,65},{2,98}... | collective-permute-start | bytes 1572872 | tf_op jit(solution)/shard_map/ppermute | solution.py:334
  126.1 15.1 %collective-permute-start.10 = (bf16[64,16,256]{2,1,0:T(8,128)(2,1)}, bf16[64,16,256]{2,1,0:T(8,128)(2,1)S(1)}, u32[]{:S(2)}, u32[]{:S(2)}) collective-permute-start(bf16[64,16,256]{2,1,0:T(8,128)(2,1)} %collective-permute-done.6.refs_0_), channel_id=1, source_target_pairs={{0,32},{32,64},{64,96},{96,0},{1,33},{33,65},{65,97},{97,1},{2,34}... | collective-permute-start | bytes 1572872 | tf_op jit(solution)/shard_map/ppermute | solution.py:331
  127.3 13.9 %collective-permute-start.11 = (bf16[64,16,256]{2,1,0:T(8,128)(2,1)}, bf16[64,16,256]{2,1,0:T(8,128)(2,1)S(1)}, u32[]{:S(2)}, u32[]{:S(2)}) collective-permute-start(bf16[64,16,256]{2,1,0:T(8,128)(2,1)} %collective-permute-done.7.refs_3_), channel_id=1, source_target_pairs={{0,96},{32,0},{64,32},{96,64},{1,97},{33,1},{65,33},{97,65},{2,98}... | collective-permute-start | bytes 1572872 | tf_op jit(solution)/shard_map/ppermute | solution.py:334
  141.2 0.8 copy-start.10
  141.2 1.0 copy-start.11
  142.2 42.5 %copy-start = (bf16[128,16,256]{2,1,0:T(8,128)(2,1)S(1)}, bf16[128,16,256]{2,1,0:T(8,128)(2,1)}, u32[]{:S(2)}) copy-start(bf16[128,16,256]{2,1,0:T(8,128)(2,1)} %experts.3.a0.b0) | copy-start | bytes 3145732
  142.2 13.1 %collective-permute-start.12 = (bf16[64,16,256]{2,1,0:T(8,128)(2,1)}, bf16[64,16,256]{2,1,0:T(8,128)(2,1)S(1)}, u32[]{:S(2)}, u32[]{:S(2)}) collective-permute-start(bf16[64,16,256]{2,1,0:T(8,128)(2,1)} %get-tuple-element.41), channel_id=1, source_target_pairs={{0,96},{32,0},{64,32},{96,64},{1,97},{33,1},{65,33},{97,65},{2,98}... | collective-permute-start | bytes 1572872 | tf_op jit(solution)/shard_map/ppermute | solution.py:334
  144.3 13.6 %collective-permute-start.13 = (bf16[64,16,256]{2,1,0:T(8,128)(2,1)}, bf16[64,16,256]{2,1,0:T(8,128)(2,1)}, u32[]{:S(2)}, u32[]{:S(2)}) collective-permute-start(bf16[64,16,256]{2,1,0:T(8,128)(2,1)} %get-tuple-element.42), channel_id=1, source_target_pairs={{0,32},{32,64},{64,96},{96,0},{1,33},{33,65},{65,97},{97,1},{2,34}... | collective-permute-start | bytes 1572872 | tf_op jit(solution)/shard_map/ppermute | solution.py:331
  158.0 11.4 %collective-permute-start.14 = (bf16[64,16,256]{2,1,0:T(8,128)(2,1)}, bf16[64,16,256]{2,1,0:T(8,128)(2,1)S(1)}, u32[]{:S(2)}, u32[]{:S(2)}) collective-permute-start(bf16[64,16,256]{2,1,0:T(8,128)(2,1)} %get-tuple-element.49), channel_id=1, source_target_pairs={{0,96},{32,0},{64,32},{96,64},{1,97},{33,1},{65,33},{97,65},{2,98}... | collective-permute-start | bytes 1572872 | tf_op jit(solution)/shard_map/ppermute | solution.py:334
  158.2 12.6 %collective-permute-start.15 = (bf16[64,16,256]{2,1,0:T(8,128)(2,1)}, bf16[64,16,256]{2,1,0:T(8,128)(2,1)S(1)}, u32[]{:S(2)}, u32[]{:S(2)}) collective-permute-start(bf16[64,16,256]{2,1,0:T(8,128)(2,1)} %get-tuple-element.51), channel_id=1, source_target_pairs={{0,32},{32,64},{64,96},{96,0},{1,33},{33,65},{65,97},{97,1},{2,34}... | collective-permute-start | bytes 1572872 | tf_op jit(solution)/shard_map/ppermute | solution.py:331
  170.8 1.0 copy-start.1
  171.8 1.0 copy-start.2
  173.1 11.6 %collective-permute-start.16 = (bf16[64,16,256]{2,1,0:T(8,128)(2,1)S(1)}, bf16[64,16,256]{2,1,0:T(8,128)(2,1)S(1)}, u32[]{:S(2)}, u32[]{:S(2)}) collective-permute-start(bf16[64,16,256]{2,1,0:T(8,128)(2,1)S(1)} %get-tuple-element.52), channel_id=1, source_target_pairs={{0,32},{32,64},{64,96},{96,0},{1,33},{33,65},{65,97},{97,1},{2,34}... | collective-permute-start | bytes 1572872 | tf_op jit(solution)/shard_map/ppermute | solution.py:331
  173.2 49.7 %copy-start.7 = (f32[8,6]{1,0:T(8,128)S(1)}, f32[8,6]{1,0:T(8,128)}, u32[]{:S(2)}) copy-start(f32[8,6]{1,0:T(8,128)} %gates.1) | copy-start | bytes 580
  173.2 11.5 %collective-permute-start.17 = (bf16[64,16,256]{2,1,0:T(8,128)(2,1)S(1)}, bf16[64,16,256]{2,1,0:T(8,128)(2,1)S(1)}, u32[]{:S(2)}, u32[]{:S(2)}) collective-permute-start(bf16[64,16,256]{2,1,0:T(8,128)(2,1)S(1)} %get-tuple-element.53), channel_id=1, source_target_pairs={{0,96},{32,0},{64,32},{96,64},{1,97},{33,1},{65,33},{97,65},{2,98}... | collective-permute-start | bytes 1572872 | tf_op jit(solution)/shard_map/ppermute | solution.py:334

commit v4 on v3

--- a/solution.py
+++ b/solution.py
@@ -246,6 +246,7 @@
         in_specs=[VMEM, VMEM],
         out_specs=ANY,
         scratch_shapes=[pltpu.VMEM((shard, 2 * head), bf16), pltpu.SemaphoreType.DMA((n_ctx,))],
+        compiler_params=pltpu.CompilerParams(vmem_limit_bytes=8 * 1024 * 1024),
         name="pack",
     )(keys, values)
     everyone = lax.all_to_all(copies, CTX, 0, 0, tiled=True)

time: 225 us -> 226 us (level)
    unnamed x24 -> x28, local copies, waits for them, and re-layouts: 3.09 us -> 4.77 us
where the time goes in v4:
time: 226 us; the launch traced here: 225 us
  blocking collectives  99.5 us (44%)
  waiting for transfers between devices  60.5 us (27%)
  Pallas kernels  31.2 us (14%)
  starting transfers between devices  28.1 us (12%)
  local copies, waits for them, and re-layouts  5.82 us (3%)
    all_to_all x2, blocking collectives, home(): return lax.all_to_all(rows, HOME, 0, 0, tiled=True)  73 us
    ppermute x6, waiting for transfers between devices, up(): return lax.ppermute(rows, 'y', shift(1, 4))  28 us
    all_to_all x1, blocking collectives, on_device(): lax.all_to_all(term.reshape(-1, tokens, quarter), EXP, 0, 0, tiled=True)  26.5 us
    pallas_call x3, Pallas kernels, expert_call(): pl.pallas_call(functools.partial(expert_kernel, sizes_in, sizes_out), out...  24.8 us
    ppermute x6, waiting for transfers between devices, down(): return lax.ppermute(rows, 'y', shift(-1, 4))  13.7 us
    all_to_all x1, waiting for transfers between devices, on_device(): everyone = lax.all_to_all(copies, CTX, 0, 0, tiled=True)  11.5 us
    ppermute x6, starting transfers between devices, down(): return lax.ppermute(rows, 'y', shift(-1, 4))  10.7 us
    ppermute x3, waiting for transfers between devices, on_device(): weights.append(cols if d == 0 else lax.ppermute(cols, QUAD, flip(d)))  5.97 us
  transfers between devices with their start and end apart: 19, of which 13 were waited for; matrix products, arithmetic and copies ran while one was open for 0% of the time, Pallas kernels for 11%

profile of v4, /device:TPU:3, one launch (start us, length us, event | category | flops | bytes accessed | tf_op | source)
XLA Modules:
  0.0 225.2 jit_solution(12435614481334673824)
XLA Ops:
  1.7 1.1 pack.1
  2.8 5.8 %all-to-all-start = ((bf16[8,256,256]{2,1,0:T(8,128)(2,1)}), bf16[8,256,256]{2,1,0:T(8,128)(2,1)S(1)}, u32[]{:S(2)}, u32[]{:S(2)}) async-start(bf16[8,256,256]{2,1,0:T(8,128)(2,1)} %pack.1), calls=%async_computation | async-start | bytes 2097152 | tf_op jit(solution)/shard_map/all_to_all | solution.py:252
  8.7 1.0 collective-permute-start.3
  9.7 1.2 collective-permute-start.4
  11.4 11.5 %all-to-all-done.kv_at = bf16[8,256,256]{2,1,0:T(8,128)(2,1)S(1)} async-done(((bf16[8,256,256]{2,1,0:T(8,128)(2,1)}), bf16[8,256,256]{2,1,0:T(8,128)(2,1)S(1)}, u32[]{:S(2)}, u32[]{:S(2)}) %all-to-all-start) | async-done | bytes 1048608 | tf_op jit(solution)/shard_map/all_to_all | solution.py:252
  23.6 3.4 %collective-permute-start = (bf16[256,128]{1,0:T(8,128)(2,1)S(1)}, bf16[256,128]{1,0:T(8,128)(2,1)S(1)}, u32[]{:S(2)}, u32[]{:S(2)}) collective-permute-start(bf16[256,128]{1,0:T(8,128)(2,1)S(1)} %attention.1.a0), channel_id=1, source_target_pairs={{0,1},{1,0},{2,3},{3,2},{4,5},{5,4},{6,7},{7,6},{8,9},{9,8},{10,11... | collective-permute-start | bytes 196616 | tf_op jit(solution)/shard_map/ppermute | solution.py:266
  28.8 6.0 %collective-permute-done.5.w3 = bf16[128,1024]{1,0:T(8,128)(2,1)S(1)} collective-permute-done((bf16[128,1024]{1,0:T(8,128)(2,1)S(1)}, bf16[128,1024]{1,0:T(8,128)(2,1)S(1)}, u32[]{:S(2)}, u32[]{:S(2)}) %collective-permute-start.5) | collective-permute-done | bytes 262176 | tf_op jit(solution)/shard_map/ppermute | solution.py:241
  34.8 1.4 collective-permute-done.2.a3
  36.6 26.5 %all_to_all.20.terms = bf16[32,8,1024]{2,1,0:T(8,128)(2,1)S(1)} all-to-all(bf16[32,8,1024]{2,1,0:T(8,128)(2,1)S(1)} %bitcast.12), channel_id=1, replica_groups=mesh['xh'=2,'y'=4,'z'=8,'xl'=2,'core'=2] {'z','xl','core'}, dimensions={0} | all-to-all | bytes 1048576 | tf_op jit(solution)/shard_map/all_to_all | solution.py:275
  64.0 36.2 %all_to_all.21 = bf16[64,32,256]{2,1,0:T(8,128)(2,1)S(1)} all-to-all(bf16[64,32,256]{2,1,0:T(8,128)(2,1)S(1)} %bitcast.13), channel_id=1, replica_groups=mesh['xh'=2,'y'=4,'z'=8,'xl'=2,'core'=2] {'xh','z','xl','core'}, dimensions={0} | all-to-all | bytes 2097152 | tf_op jit(solution)/shard_map/all_to_all | solution.py:295
  101.2 1.2 collective-permute-start.6
  102.4 1.5 collective-permute-start.7
  103.9 2.7 %collective-permute-start.9 = (bf16[64,16,256]{2,1,0:T(8,128)(2,1)S(1)}, bf16[64,16,256]{2,1,0:T(8,128)(2,1)}, u32[]{:S(2)}, u32[]{:S(2)}) collective-permute-start(bf16[64,16,256]{2,1,0:T(8,128)(2,1)S(1)} %bitcast.26), channel_id=1, source_target_pairs={{0,96},{32,0},{64,32},{96,64},{1,97},{33,1},{65,33},{97,65},{2,98}... | collective-permute-start | bytes 1572872 | tf_op jit(solution)/shard_map/ppermute | solution.py:335
  106.6 8.1 %experts.3.a0.b0 = bf16[128,16,256]{2,1,0:T(8,128)(2,1)} custom-call(bf16[128,16,256]{2,1,0:T(8,128)(2,1)} %bitcast.24, bf16[352,4096]{1,0:T(8,128)(2,1)} %bitcast.15, bf16[352,4096]{1,0:T(8,128)(2,1)} %bitcast.18, bf16[352,4096]{1,0:T(8,128)(2,1)} %bitcast.21), custom_call_target="tpu_custom_call" | custom-call | flops 1107296256 | bytes 8650752 | tf_op jit(solution)/shard_map/experts/pallas_call | solution.py:305
  114.6 1.8 collective-permute-done.6.refs_0_
  116.6 9.7 %collective-permute-done.8.refs_1_ = bf16[64,16,256]{2,1,0:T(8,128)(2,1)} collective-permute-done((bf16[64,16,256]{2,1,0:T(8,128)(2,1)}, bf16[64,16,256]{2,1,0:T(8,128)(2,1)}, u32[]{:S(2)}, u32[]{:S(2)}) %collective-permute-start.8) | collective-permute-done | bytes 524320 | tf_op jit(solution)/shard_map/ppermute | solution.py:332
  126.8 1.2 collective-permute-start.10
  128.0 1.5 collective-permute-start.11
  129.5 8.9 %experts.4 = (bf16[64,16,256]{2,1,0:T(8,128)(2,1)}, bf16[64,16,256]{2,1,0:T(8,128)(2,1)}, bf16[64,16,256]{2,1,0:T(8,128)(2,1)}, bf16[64,16,256]{2,1,0:T(8,128)(2,1)}) custom-call(bf16[64,16,256]{2,1,0:T(8,128)(2,1)} %collective-permute-done.6.refs_0_, bf16[64,16,256]{2,1,0:T(8,128)(2,1)} %collective-permute-done.8.refs_1_, ...), custom_call_target="tpu_custom_call" | custom-call | flops 2214592512 | bytes 8650752 | tf_op jit(solution)/shard_map/experts/pallas_call | solution.py:305
  138.4 3.5 %collective-permute-done.10.refs_0_ = bf16[64,16,256]{2,1,0:T(8,128)(2,1)S(1)} collective-permute-done((bf16[64,16,256]{2,1,0:T(8,128)(2,1)}, bf16[64,16,256]{2,1,0:T(8,128)(2,1)S(1)}, u32[]{:S(2)}, u32[]{:S(2)}) %collective-permute-start.10) | collective-permute-done | bytes 524320 | tf_op jit(solution)/shard_map/ppermute | solution.py:332
  142.9 2.2 collective-permute-start.12
  145.1 7.8 %experts.5 = (bf16[64,16,256]{2,1,0:T(8,128)(2,1)}, bf16[64,16,256]{2,1,0:T(8,128)(2,1)}) custom-call(bf16[64,16,256]{2,1,0:T(8,128)(2,1)} %copy-done.12, bf16[64,16,256]{2,1,0:T(8,128)(2,1)} %copy-done.13, bf16[352,4096]{1,0:T(8,128)(2,1)} %bitcast.17, bf16[352,4096]{1,0:T(8,128)(2,1)} %bitcast.20, bf16[352,4096]{1,0:T(8,128)(2,1)} %bitcast.23), custom_call_target="tpu_custom_call" | custom-call | flops 1107296256 | bytes 8650752 | tf_op jit(solution)/shard_map/experts/pallas_call | solution.py:305
  152.9 3.1 %collective-permute-done.12.a1 = bf16[64,16,256]{2,1,0:T(8,128)(2,1)S(1)} collective-permute-done((bf16[64,16,256]{2,1,0:T(8,128)(2,1)}, bf16[64,16,256]{2,1,0:T(8,128)(2,1)S(1)}, u32[]{:S(2)}, u32[]{:S(2)}) %collective-permute-start.12) | collective-permute-done | bytes 524320 | tf_op jit(solution)/shard_map/ppermute | solution.py:335
  156.0 2.7 %collective-permute-done.13.b2 = bf16[64,16,256]{2,1,0:T(8,128)(2,1)} collective-permute-done((bf16[64,16,256]{2,1,0:T(8,128)(2,1)}, bf16[64,16,256]{2,1,0:T(8,128)(2,1)}, u32[]{:S(2)}, u32[]{:S(2)}) %collective-permute-start.13) | collective-permute-done | bytes 524320 | tf_op jit(solution)/shard_map/ppermute | solution.py:332
  158.9 1.3 collective-permute-start.15
  160.2 9.9 %collective-permute-done.14.from_above = bf16[64,16,256]{2,1,0:T(8,128)(2,1)S(1)} collective-permute-done((bf16[64,16,256]{2,1,0:T(8,128)(2,1)}, bf16[64,16,256]{2,1,0:T(8,128)(2,1)S(1)}, u32[]{:S(2)}, u32[]{:S(2)}) %collective-permute-start.14) | collective-permute-done | bytes 524320 | tf_op jit(solution)/shard_map/ppermute | solution.py:335
  170.1 1.4 collective-permute-done.15.from_below
  173.9 2.7 %collective-permute-start.17 = (bf16[64,16,256]{2,1,0:T(8,128)(2,1)S(1)}, bf16[64,16,256]{2,1,0:T(8,128)(2,1)S(1)}, u32[]{:S(2)}, u32[]{:S(2)}) collective-permute-start(bf16[64,16,256]{2,1,0:T(8,128)(2,1)S(1)} %get-tuple-element.53), channel_id=1, source_target_pairs={{0,96},{32,0},{64,32},{96,64},{1,97},{33,1},{65,33},{97,65},{2,98}... | collective-permute-start | bytes 1572872 | tf_op jit(solution)/shard_map/ppermute | solution.py:335
  176.6 8.8 %collective-permute-done.16.a2 = bf16[64,16,256]{2,1,0:T(8,128)(2,1)S(1)} collective-permute-done((bf16[64,16,256]{2,1,0:T(8,128)(2,1)S(1)}, bf16[64,16,256]{2,1,0:T(8,128)(2,1)S(1)}, u32[]{:S(2)}, u32[]{:S(2)}) %collective-permute-start.16) | collective-permute-done | bytes 524320 | tf_op jit(solution)/shard_map/ppermute | solution.py:332
  185.4 1.4 totals.1
  186.8 36.8 %all_to_all.22.routed = bf16[64,32,256]{2,1,0:T(8,128)(2,1)S(1)} all-to-all(bf16[64,32,256]{2,1,0:T(8,128)(2,1)S(1)} %bitcast.11), channel_id=1, replica_groups=mesh['xh'=2,'y'=4,'z'=8,'xl'=2,'core'=2] {'xh','z','xl','core'}, dimensions={0} | all-to-all | bytes 2097152 | tf_op jit(solution)/shard_map/all_to_all | solution.py:295
  223.6 1.6 combine.1
  (49 shorter events, 11.3 us)
Async XLA Ops:
  0.0 0.8 copy-start.3
  0.8 0.8 copy-start.4
  1.7 6.9 %copy-start.11 = (bf16[128,4096]{1,0:T(8,128)(2,1)S(1)}, bf16[128,4096]{1,0:T(8,128)(2,1)}, u32[]{:S(2)}) copy-start(bf16[128,4096]{1,0:T(8,128)(2,1)} %param.15) | copy-start | bytes 3145732
  1.7 21.2 %copy-start.5 = (bf16[256,128]{1,0:T(8,128)(2,1)S(1)}, bf16[256,128]{1,0:T(8,128)(2,1)}, u32[]{:S(2)}) copy-start(bf16[256,128]{1,0:T(8,128)(2,1)} %q_ref.1) | copy-start | bytes 196612
  2.8 20.1 %all-to-all-start = ((bf16[8,256,256]{2,1,0:T(8,128)(2,1)}), bf16[8,256,256]{2,1,0:T(8,128)(2,1)S(1)}, u32[]{:S(2)}, u32[]{:S(2)}) async-start(bf16[8,256,256]{2,1,0:T(8,128)(2,1)} %pack.1), calls=%async_computation | async-start | bytes 2097152 | tf_op jit(solution)/shard_map/all_to_all | solution.py:252
  8.5 54.5 %copy-start.6 = (bf16[8,4096]{1,0:T(8,128)(2,1)S(1)}, bf16[8,4096]{1,0:T(8,128)(2,1)}, u32[]{:S(2)}) copy-start(bf16[8,4096]{1,0:T(8,128)(2,1)} %stream.1) | copy-start | bytes 196612
  8.5 54.5 %copy-start.7 = (s32[8,6]{1,0:T(8,128)S(1)}, s32[8,6]{1,0:T(8,128)}, u32[]{:S(2)}) copy-start(s32[8,6]{1,0:T(8,128)} %ids.3) | copy-start | bytes 580
  8.6 54.5 %copy-start.8 = (f32[4096]{0:T(1024)S(1)}, f32[4096]{0:T(1024)}, u32[]{:S(2)}) copy-start(f32[4096]{0:T(1024)} %param.16) | copy-start | bytes 49156
  8.7 19.4 %collective-permute-start.3 = (bf16[128,1024]{1,0:T(8,128)(2,1)S(1)}, bf16[128,1024]{1,0:T(8,128)(2,1)S(1)}, u32[]{:S(2)}, u32[]{:S(2)}) collective-permute-start(bf16[128,1024]{1,0:T(8,128)(2,1)S(1)} %get-tuple-element.58), channel_id=1, source_target_pairs={{0,1},{1,0},{2,3},{3,2},{4,5},{5,4},{6,7},{7,6},{8,9},{9,8},{10,11... | collective-permute-start | bytes 786440 | tf_op jit(solution)/shard_map/ppermute | solution.py:241
  9.7 19.1 %collective-permute-start.4 = (bf16[128,1024]{1,0:T(8,128)(2,1)S(1)}, bf16[128,1024]{1,0:T(8,128)(2,1)S(1)}, u32[]{:S(2)}, u32[]{:S(2)}) collective-permute-start(bf16[128,1024]{1,0:T(8,128)(2,1)S(1)} %get-tuple-element.60), channel_id=1, source_target_pairs={{0,2},{1,3},{2,0},{3,1},{4,6},{5,7},{6,4},{7,5},{8,10},{9,11},{10,... | collective-permute-start | bytes 786440 | tf_op jit(solution)/shard_map/ppermute | solution.py:241
  10.9 23.9 %collective-permute-start.5 = (bf16[128,1024]{1,0:T(8,128)(2,1)S(1)}, bf16[128,1024]{1,0:T(8,128)(2,1)S(1)}, u32[]{:S(2)}, u32[]{:S(2)}) collective-permute-start(bf16[128,1024]{1,0:T(8,128)(2,1)S(1)} %get-tuple-element.57), channel_id=1, source_target_pairs={{0,3},{1,2},{2,1},{3,0},{4,7},{5,6},{6,5},{7,4},{8,11},{9,10},{10,... | collective-permute-start | bytes 786440 | tf_op jit(solution)/shard_map/ppermute | solution.py:241
  23.6 11.1 %collective-permute-start = (bf16[256,128]{1,0:T(8,128)(2,1)S(1)}, bf16[256,128]{1,0:T(8,128)(2,1)S(1)}, u32[]{:S(2)}, u32[]{:S(2)}) collective-permute-start(bf16[256,128]{1,0:T(8,128)(2,1)S(1)} %attention.1.a0), channel_id=1, source_target_pairs={{0,1},{1,0},{2,3},{3,2},{4,5},{5,4},{6,7},{7,6},{8,9},{9,8},{10,11... | collective-permute-start | bytes 196616 | tf_op jit(solution)/shard_map/ppermute | solution.py:266
  27.0 7.7 %collective-permute-start.1 = (bf16[256,128]{1,0:T(8,128)(2,1)S(1)}, bf16[256,128]{1,0:T(8,128)(2,1)S(1)}, u32[]{:S(2)}, u32[]{:S(2)}) collective-permute-start(bf16[256,128]{1,0:T(8,128)(2,1)S(1)} %attention.1.a0), channel_id=1, source_target_pairs={{0,2},{1,3},{2,0},{3,1},{4,6},{5,7},{6,4},{7,5},{8,10},{9,11},{10,... | collective-permute-start | bytes 196616 | tf_op jit(solution)/shard_map/ppermute | solution.py:266
  28.0 8.1 %collective-permute-start.2 = (bf16[256,128]{1,0:T(8,128)(2,1)S(1)}, bf16[256,128]{1,0:T(8,128)(2,1)S(1)}, u32[]{:S(2)}, u32[]{:S(2)}) collective-permute-start(bf16[256,128]{1,0:T(8,128)(2,1)S(1)} %attention.1.a0), channel_id=1, source_target_pairs={{0,3},{1,2},{2,1},{3,0},{4,7},{5,6},{6,5},{7,4},{8,11},{9,10},{10,... | collective-permute-start | bytes 196616 | tf_op jit(solution)/shard_map/ppermute | solution.py:266
  100.2 6.3 %copy-start.10 = (bf16[64,32,256]{2,1,0:T(8,128)(2,1)}, bf16[64,32,256]{2,1,0:T(8,128)(2,1)S(1)}, u32[]{:S(2)}) copy-start(bf16[64,32,256]{2,1,0:T(8,128)(2,1)S(1)} %all_to_all.21) | copy-start | bytes 3145732
  101.2 15.3 %collective-permute-start.6 = (bf16[64,16,256]{2,1,0:T(8,128)(2,1)S(1)}, bf16[64,16,256]{2,1,0:T(8,128)(2,1)}, u32[]{:S(2)}, u32[]{:S(2)}) collective-permute-start(bf16[64,16,256]{2,1,0:T(8,128)(2,1)S(1)} %bitcast.25), channel_id=1, source_target_pairs={{0,32},{32,64},{64,96},{96,0},{1,33},{33,65},{65,97},{97,1},{2,34}... | collective-permute-start | bytes 1572872 | tf_op jit(solution)/shard_map/ppermute | solution.py:332
  102.4 14.2 %collective-permute-start.7 = (bf16[64,16,256]{2,1,0:T(8,128)(2,1)}, bf16[64,16,256]{2,1,0:T(8,128)(2,1)}, u32[]{:S(2)}, u32[]{:S(2)}) collective-permute-start(bf16[64,16,256]{2,1,0:T(8,128)(2,1)} %bitcast.5), channel_id=1, source_target_pairs={{0,96},{32,0},{64,32},{96,64},{1,97},{33,1},{65,33},{97,65},{2,98}... | collective-permute-start | bytes 1572872 | tf_op jit(solution)/shard_map/ppermute | solution.py:335
  103.9 22.5 %collective-permute-start.8 = (bf16[64,16,256]{2,1,0:T(8,128)(2,1)}, bf16[64,16,256]{2,1,0:T(8,128)(2,1)}, u32[]{:S(2)}, u32[]{:S(2)}) collective-permute-start(bf16[64,16,256]{2,1,0:T(8,128)(2,1)} %bitcast.5), channel_id=1, source_target_pairs={{0,32},{32,64},{64,96},{96,0},{1,33},{33,65},{65,97},{97,1},{2,34}... | collective-permute-start | bytes 1572872 | tf_op jit(solution)/shard_map/ppermute | solution.py:332
  103.9 22.9 %collective-permute-start.9 = (bf16[64,16,256]{2,1,0:T(8,128)(2,1)S(1)}, bf16[64,16,256]{2,1,0:T(8,128)(2,1)}, u32[]{:S(2)}, u32[]{:S(2)}) collective-permute-start(bf16[64,16,256]{2,1,0:T(8,128)(2,1)S(1)} %bitcast.26), channel_id=1, source_target_pairs={{0,96},{32,0},{64,32},{96,64},{1,97},{33,1},{65,33},{97,65},{2,98}... | collective-permute-start | bytes 1572872 | tf_op jit(solution)/shard_map/ppermute | solution.py:335
  126.8 15.1 %collective-permute-start.10 = (bf16[64,16,256]{2,1,0:T(8,128)(2,1)}, bf16[64,16,256]{2,1,0:T(8,128)(2,1)S(1)}, u32[]{:S(2)}, u32[]{:S(2)}) collective-permute-start(bf16[64,16,256]{2,1,0:T(8,128)(2,1)} %collective-permute-done.6.refs_0_), channel_id=1, source_target_pairs={{0,32},{32,64},{64,96},{96,0},{1,33},{33,65},{65,97},{97,1},{2,34}... | collective-permute-start | bytes 1572872 | tf_op jit(solution)/shard_map/ppermute | solution.py:332
  128.0 13.9 %collective-permute-start.11 = (bf16[64,16,256]{2,1,0:T(8,128)(2,1)}, bf16[64,16,256]{2,1,0:T(8,128)(2,1)S(1)}, u32[]{:S(2)}, u32[]{:S(2)}) collective-permute-start(bf16[64,16,256]{2,1,0:T(8,128)(2,1)} %collective-permute-done.7.refs_3_), channel_id=1, source_target_pairs={{0,96},{32,0},{64,32},{96,64},{1,97},{33,1},{65,33},{97,65},{2,98}... | collective-permute-start | bytes 1572872 | tf_op jit(solution)/shard_map/ppermute | solution.py:335
  141.9 1.0 copy-start.13
  142.9 42.5 %copy-start = (bf16[128,16,256]{2,1,0:T(8,128)(2,1)S(1)}, bf16[128,16,256]{2,1,0:T(8,128)(2,1)}, u32[]{:S(2)}) copy-start(bf16[128,16,256]{2,1,0:T(8,128)(2,1)} %experts.3.a0.b0) | copy-start | bytes 3145732
  142.9 13.1 %collective-permute-start.12 = (bf16[64,16,256]{2,1,0:T(8,128)(2,1)}, bf16[64,16,256]{2,1,0:T(8,128)(2,1)S(1)}, u32[]{:S(2)}, u32[]{:S(2)}) collective-permute-start(bf16[64,16,256]{2,1,0:T(8,128)(2,1)} %get-tuple-element.41), channel_id=1, source_target_pairs={{0,96},{32,0},{64,32},{96,64},{1,97},{33,1},{65,33},{97,65},{2,98}... | collective-permute-start | bytes 1572872 | tf_op jit(solution)/shard_map/ppermute | solution.py:335
  145.1 13.6 %collective-permute-start.13 = (bf16[64,16,256]{2,1,0:T(8,128)(2,1)}, bf16[64,16,256]{2,1,0:T(8,128)(2,1)}, u32[]{:S(2)}, u32[]{:S(2)}) collective-permute-start(bf16[64,16,256]{2,1,0:T(8,128)(2,1)} %get-tuple-element.42), channel_id=1, source_target_pairs={{0,32},{32,64},{64,96},{96,0},{1,33},{33,65},{65,97},{97,1},{2,34}... | collective-permute-start | bytes 1572872 | tf_op jit(solution)/shard_map/ppermute | solution.py:332
  158.7 11.4 %collective-permute-start.14 = (bf16[64,16,256]{2,1,0:T(8,128)(2,1)}, bf16[64,16,256]{2,1,0:T(8,128)(2,1)S(1)}, u32[]{:S(2)}, u32[]{:S(2)}) collective-permute-start(bf16[64,16,256]{2,1,0:T(8,128)(2,1)} %get-tuple-element.49), channel_id=1, source_target_pairs={{0,96},{32,0},{64,32},{96,64},{1,97},{33,1},{65,33},{97,65},{2,98}... | collective-permute-start | bytes 1572872 | tf_op jit(solution)/shard_map/ppermute | solution.py:335
  158.9 12.6 %collective-permute-start.15 = (bf16[64,16,256]{2,1,0:T(8,128)(2,1)}, bf16[64,16,256]{2,1,0:T(8,128)(2,1)S(1)}, u32[]{:S(2)}, u32[]{:S(2)}) collective-permute-start(bf16[64,16,256]{2,1,0:T(8,128)(2,1)} %get-tuple-element.51), channel_id=1, source_target_pairs={{0,32},{32,64},{64,96},{96,0},{1,33},{33,65},{65,97},{97,1},{2,34}... | collective-permute-start | bytes 1572872 | tf_op jit(solution)/shard_map/ppermute | solution.py:332
  171.5 1.0 copy-start.1
  172.6 1.0 copy-start.2
  173.8 11.6 %collective-permute-start.16 = (bf16[64,16,256]{2,1,0:T(8,128)(2,1)S(1)}, bf16[64,16,256]{2,1,0:T(8,128)(2,1)S(1)}, u32[]{:S(2)}, u32[]{:S(2)}) collective-permute-start(bf16[64,16,256]{2,1,0:T(8,128)(2,1)S(1)} %get-tuple-element.52), channel_id=1, source_target_pairs={{0,32},{32,64},{64,96},{96,0},{1,33},{33,65},{65,97},{97,1},{2,34}... | collective-permute-start | bytes 1572872 | tf_op jit(solution)/shard_map/ppermute | solution.py:332
  173.9 49.7 %copy-start.9 = (f32[8,6]{1,0:T(8,128)S(1)}, f32[8,6]{1,0:T(8,128)}, u32[]{:S(2)}) copy-start(f32[8,6]{1,0:T(8,128)} %gates.1) | copy-start | bytes 580
  173.9 11.5 %collective-permute-start.17 = (bf16[64,16,256]{2,1,0:T(8,128)(2,1)S(1)}, bf16[64,16,256]{2,1,0:T(8,128)(2,1)S(1)}, u32[]{:S(2)}, u32[]{:S(2)}) collective-permute-start(bf16[64,16,256]{2,1,0:T(8,128)(2,1)S(1)} %get-tuple-element.53), channel_id=1, source_target_pairs={{0,96},{32,0},{64,32},{96,64},{1,97},{33,1},{65,33},{97,65},{2,98}... | collective-permute-start | bytes 1572872 | tf_op jit(solution)/shard_map/ppermute | solution.py:335
  (1 other events, 0.8 us)
